TPU v7x, 32 devices: a whole 2x2x4 slice. The times are simulated.
32 devices in a mesh: row: 4 (over x, core), col: 2 (over y), depth: 4 (over z).
Axes of the slice: x: 2, y: 2, z: 4, core: 2. Of those that a mesh axis runs over, the one named last changes fastest.
Arguments:
- tokens: bfloat16 [1024, 12288], P(('row', 'col'), 'depth'), may hold values from -6 to 6
- w_qkv: bfloat16 [12288, 64, 3, 128], P('depth', ('row', 'col')), may hold values from -0.0546875 to 0.0546875
- w_out: bfloat16 [64, 128, 12288], P(('row', 'col'), None, 'depth'), may hold values from -0.125 to 0.125
- positions: int32 [1024], P('depth'), may hold values from 0 to 255, as said below
- d_output: bfloat16 [1024, 12288], P(('row', 'col'), 'depth'), may hold values from -1.5 to 1.5
Outputs:
- output: bfloat16 [1024, 12288], P(('row', 'col'), 'depth')
- d_tokens: bfloat16 [1024, 12288], P(('row', 'col'), 'depth')
- d_qkv_weight: float32 [12288, 64, 3, 128], P('depth', ('row', 'col'))
- d_out_weight: float32 [64, 128, 12288], P(('row', 'col'), None, 'depth')
Inputs may be any that keep to these rules, and one draw needn't show every extreme that they name: Within each sequence of 256 tokens the positions start at 0 on its first token and either rise by one from token to token or fall back to 0 where a new document begins; in some sequence one document fills all 256 tokens.
All inputs are finite; a program needn't handle non-finite values.
Results may differ from a plain program's by a relative error of at most 0.03.
Values may be sent and summed in bfloat16 or wider, within the bound.
A program may use at most 192 MiB of HBM per device.

v0:
```python
import math

import jax
import jax.numpy as jnp
from jax import lax
from jax.sharding import PartitionSpec as P


def allowed_pairs(seq_positions):
    places = jnp.arange(seq_positions.shape[0], dtype=jnp.int32)
    earlier = places[None, :] <= places[:, None]
    inside = places[None, :] >= (places - seq_positions)[:, None]
    return earlier & inside


def attend(queries, key_rows, value_rows, allowed, score_scale):
    scores = (
        jnp.einsum("ihd,jhd->hij", queries, key_rows, preferred_element_type=jnp.float32)
        * score_scale
    )
    weights = jnp.where(allowed[None], jnp.exp(scores), 0.0)
    probabilities = weights / jnp.sum(weights, axis=-1, keepdims=True)
    rounded = probabilities.astype(jnp.bfloat16)
    mixed_heads = jnp.einsum(
        "hij,jhd->ihd", rounded, value_rows, preferred_element_type=jnp.float32
    ).astype(jnp.bfloat16)
    return (mixed_heads, probabilities, rounded)


def attend_back(queries, key_rows, value_rows, probabilities, rounded, d_mixed, score_scale):
    d_probs = jnp.einsum("ihd,jhd->hij", d_mixed, value_rows, preferred_element_type=jnp.float32)
    row_delta = jnp.sum(probabilities * d_probs, axis=-1, keepdims=True)
    d_scores = (probabilities * (d_probs - row_delta) * score_scale).astype(jnp.bfloat16)
    grad_query = jnp.einsum("hij,jhd->ihd", d_scores, key_rows, preferred_element_type=jnp.float32)
    grad_key = jnp.einsum("hij,ihd->jhd", d_scores, queries, preferred_element_type=jnp.float32)
    grad_value = jnp.einsum("hij,ihd->jhd", rounded, d_mixed, preferred_element_type=jnp.float32)
    return jnp.stack([grad_query, grad_key, grad_value], axis=2).astype(jnp.bfloat16)


def gather_rows(local_rows):
    gathered = lax.all_gather(local_rows, ("row", "col"), axis=0, tiled=True)
    return gathered


def per_device(tokens, w_qkv, w_out, positions, d_output):
    seq_len = positions.shape[0]
    local_heads = w_qkv.shape[1]
    head_size = w_qkv.shape[3]
    width_part = w_qkv.shape[0]
    score_scale = 1.0 / math.sqrt(head_size)
    qkv_flat = w_qkv.reshape(width_part, local_heads * 3 * head_size)
    out_flat = w_out.reshape(local_heads * head_size, width_part)
    contract_first = (((0,), (0,)), ((), ()))
    contract_last = (((1,), (1,)), ((), ()))
    gathered = gather_rows(tokens)
    piece = gathered
    projected = lax.psum_scatter(
        jnp.dot(piece, qkv_flat, preferred_element_type=jnp.float32),
        "depth",
        scatter_dimension=0,
        tiled=True,
    )
    projected = projected.astype(jnp.bfloat16).reshape(seq_len, local_heads, 3, head_size)
    queries = projected[:, :, 0]
    key_rows = projected[:, :, 1]
    value_rows = projected[:, :, 2]
    allowed = allowed_pairs(positions)
    mixed_heads, probabilities, rounded = attend(
        queries, key_rows, value_rows, allowed, score_scale
    )
    heads_all = lax.all_gather(
        mixed_heads.reshape(seq_len, local_heads * head_size), "depth", axis=0, tiled=True
    )
    piece = heads_all
    output = lax.psum_scatter(
        jnp.dot(piece, out_flat, preferred_element_type=jnp.float32).astype(jnp.bfloat16),
        ("row", "col"),
        scatter_dimension=0,
        tiled=True,
    )
    grad_all = gather_rows(d_output)
    piece = grad_all
    d_mixed = lax.psum_scatter(
        lax.dot_general(piece, out_flat, contract_last, preferred_element_type=jnp.float32),
        "depth",
        scatter_dimension=0,
        tiled=True,
    )
    d_mixed = d_mixed.astype(jnp.bfloat16).reshape(seq_len, local_heads, head_size)
    d_out_weight = lax.dot_general(
        heads_all, grad_all, contract_first, preferred_element_type=jnp.float32
    )
    d_out_weight = d_out_weight.reshape(local_heads, head_size, width_part)
    d_projected = attend_back(
        queries, key_rows, value_rows, probabilities, rounded, d_mixed, score_scale
    )
    projected_grads = lax.all_gather(
        d_projected.reshape(seq_len, local_heads * 3 * head_size), "depth", axis=0, tiled=True
    )
    d_qkv_weight = lax.dot_general(
        gathered, projected_grads, contract_first, preferred_element_type=jnp.float32
    )
    d_qkv_weight = d_qkv_weight.reshape(width_part, local_heads, 3, head_size)
    piece = projected_grads
    d_tokens = lax.psum_scatter(
        lax.dot_general(piece, qkv_flat, contract_last, preferred_element_type=jnp.float32).astype(
            jnp.bfloat16
        ),
        ("row", "col"),
        scatter_dimension=0,
        tiled=True,
    )
    return (output, d_tokens, d_qkv_weight, d_out_weight)


def solution(mesh):
    in_specs = (
        P(("row", "col"), "depth"),
        P("depth", ("row", "col"), None, None),
        P(("row", "col"), None, "depth"),
        P("depth"),
        P(("row", "col"), "depth"),
    )
    out_specs = (
        P(("row", "col"), "depth"),
        P(("row", "col"), "depth"),
        P("depth", ("row", "col"), None, None),
        P(("row", "col"), None, "depth"),
    )
    return jax.shard_map(
        per_device, mesh=mesh, in_specs=in_specs, out_specs=out_specs, check_vma=False
    )
```

profile of v0, /device:TPU:0, one launch (start us, length us, event | category | flops | bytes accessed | tf_op | source)
XLA Modules:
  0.0 701.3 jit_solution(1103228835369433847)
XLA Ops:
  7.2 0.7 all-gather.5.cloned.1.call-update
  7.9 0.7 all-gather.9.cloned.1.call-update
  8.7 24.5 %copy.22 = bf16[3072,8,3,128]{0,3,2,1:T(8,128)(2,1)} copy(bf16[3072,8,3,128]{3,1,2,0:T(8,128)(2,1)} %param.6) | data formatting | bytes 37748736 | tf_op args[1]
  33.2 25.0 %all-gather.5.cloned.1.call-done = bf16[1024,3072]{1,0:T(8,128)(2,1)} async-done(((bf16[128,3072]{1,0:T(8,128)(2,1)}), bf16[1024,3072]{1,0:T(8,128)(2,1)}) %all-gather.5.cloned.1.call-update) | async-done | bytes 6291472 | tf_op jit(solution)/shard_map/all_gather | solution.py:41
  58.1 26.2 %fusion.42 = f32[1024,3072]{1,0:T(8,128)} fusion(bf16[1024,3072]{1,0:T(8,128)(2,1)} %all-gather.5.cloned.1.call-done, bf16[3072,3072]{0,1:T(8,128)(2,1)} %bitcast.61), kind=kOutput, calls=%fused_computation.36 | convolution fusion | flops 19327352832 | bytes 37748736 | tf_op jit(solution)/shard_map/dot_general | solution.py:58
  84.4 21.2 %all-gather.9.cloned.1.call-done = bf16[1024,3072]{1,0:T(8,128)(2,1)} async-done(((bf16[128,3072]{1,0:T(8,128)(2,1)}), bf16[1024,3072]{1,0:T(8,128)(2,1)}) %all-gather.9.cloned.1.call-update) | async-done | bytes 6291472 | tf_op jit(solution)/shard_map/all_gather | solution.py:41
  105.6 12.0 %fusion.43 = f32[1024,1024]{1,0:T(8,128)} fusion(bf16[1024,3072]{1,0:T(8,128)(2,1)} %all-gather.9.cloned.1.call-done, bf16[1024,3072]{1,0:T(8,128)(2,1)} %bitcast.72), kind=kOutput, calls=%fused_computation.37 | convolution fusion | flops 6442450944 | bytes 16777216 | tf_op jit(solution)/shard_map/dot_general | solution.py:84
  117.7 0.6 copy-done
  118.3 202.1 %reduce-scatter.5.cloned.1.call-done = f32[256,3072]{1,0:T(8,128)} async-done(((f32[1024,3072]{1,0:T(8,128)}), f32[256,3072]{1,0:T(8,128)}) %reduce-scatter.5.cloned.1.call-update) | async-done | bytes 3145744 | tf_op jit(solution)/shard_map/reduce_scatter | solution.py:57
  320.4 2.1 convert_element_type.29
  322.5 0.7 copy.23
  323.2 0.7 fusion.11
  323.9 1.5 convolution_convert_fusion.3
  325.4 0.2 all-gather.11.cloned.1.call-start
  325.6 74.8 %reduce-scatter.9.cloned.1.call-done = f32[256,1024]{1,0:T(8,128)} async-done(((f32[1024,1024]{1,0:T(8,128)}), f32[256,1024]{1,0:T(8,128)}) %reduce-scatter.9.cloned.1.call-update) | async-done | bytes 1048592 | tf_op jit(solution)/shard_map/reduce_scatter | solution.py:83
  400.4 1.3 convert_element_type.34
  401.7 0.2 copy.48
  401.9 1.8 fusion.29
  403.7 4.9 fusion.19
  408.6 5.2 fusion.22
  413.8 2.2 fusion.18
  416.1 0.2 pad_maximum_fusion
  416.2 1.2 copy.36
  417.6 33.4 %all-gather.7.cloned.1.call-done = bf16[1024,1024]{0,1:T(8,128)(2,1)} async-done(((bf16[256,1024]{0,1:T(8,128)(2,1)}), bf16[1024,1024]{0,1:T(8,128)(2,1)}) %all-gather.7.cloned.1.call-update) | async-done | bytes 2097168 | tf_op jit(solution)/shard_map/all_gather | solution.py:71
  450.9 11.3 %convolution_convert_fusion.1 = bf16[1024,3072]{1,0:T(8,128)(2,1)} fusion(bf16[1024,1024]{0,1:T(8,128)(2,1)} %all-gather.7.cloned.1.call-done, bf16[1024,3072]{1,0:T(8,128)(2,1)} %bitcast.73), kind=kOutput, calls=%fused_computation.2 | convolution fusion | flops 6445596672 | bytes 14680064 | tf_op jit(solution)/shard_map/dot_general | solution.py:76
  462.3 0.3 reduce-scatter.11.cloned.1.call-start
  462.6 101.8 %all-gather.11.cloned.1.call-done = bf16[1024,3072]{0,1:T(8,128)(2,1)} async-done(((bf16[256,3072]{0,1:T(8,128)(2,1)}), bf16[1024,3072]{0,1:T(8,128)(2,1)}) %all-gather.11.cloned.1.call-update) | async-done | bytes 6291472 | tf_op jit(solution)/shard_map/all_gather | solution.py:97
  564.4 26.2 %convolution_convert_fusion = bf16[1024,3072]{1,0:T(8,128)(2,1)} fusion(bf16[1024,3072]{0,1:T(8,128)(2,1)} %all-gather.11.cloned.1.call-done, bf16[3072,3072]{0,1:T(8,128)(2,1)} %bitcast.62), kind=kOutput, calls=%fused_computation.1 | convolution fusion | flops 19330498560 | bytes 31457280 | tf_op jit(solution)/shard_map/dot_general | solution.py:106
  590.6 12.6 %fusion.45 = f32[1024,3072]{1,0:T(8,128)} fusion(bf16[1024,1024]{0,1:T(8,128)(2,1)} %all-gather.7.cloned.1.call-done, bf16[1024,3072]{1,0:T(8,128)(2,1)} %all-gather.9.cloned.1.call-done), kind=kOutput, calls=%fused_computation.39 | convolution fusion | flops 6442450944 | bytes 20971520 | tf_op jit(solution)/shard_map/dot_general | solution.py:90
  603.2 25.3 %fusion.44 = f32[3072,3072]{1,0:T(8,128)} fusion(bf16[1024,3072]{0,1:T(8,128)(2,1)} %all-gather.11.cloned.1.call-done, bf16[1024,3072]{1,0:T(8,128)(2,1)S(1)} %bitcast.75), kind=kOutput, calls=%fused_computation.38 | convolution fusion | flops 19327352832 | bytes 50331648 | tf_op jit(solution)/shard_map/dot_general | solution.py:100
  628.5 37.7 %copy.37 = f32[3072,8,3,128]{3,1,2,0:T(8,128)} copy(f32[3072,8,3,128]{0,3,2,1:T(8,128)} %bitcast.60) | data formatting | bytes 75497472
  666.1 28.3 %reduce-scatter.11.cloned.1.call-done = bf16[128,3072]{1,0:T(8,128)(2,1)} async-done(((bf16[1024,3072]{1,0:T(8,128)(2,1)}), bf16[128,3072]{1,0:T(8,128)(2,1)}) %reduce-scatter.11.cloned.1.call-update) | async-done | bytes 786448 | tf_op jit(solution)/shard_map/reduce_scatter | solution.py:105
  (23 shorter events, 0.4 us)
Async XLA Ops:
  7.2 51.0 %all-gather.5.cloned.1.call-start = ((), (), s32[]{:S(2)}) async-start(), calls=%async_computation.4 | async-start | bytes 7077888 | tf_op jit(solution)/shard_map/all_gather | solution.py:41
  7.9 97.7 %all-gather.9.cloned.1.call-start = ((), (), s32[]{:S(2)}) async-start(), calls=%async_computation.8 | async-start | bytes 7077888 | tf_op jit(solution)/shard_map/all_gather | solution.py:41
  8.6 311.7 %reduce-scatter.5.cloned.1.call-start = ((), (), s32[]{:S(2)}) async-start(), calls=%async_computation.5 | async-start | bytes 15728640 | tf_op jit(solution)/shard_map/reduce_scatter | solution.py:57
  84.3 316.0 %reduce-scatter.9.cloned.1.call-start = ((), (), s32[]{:S(2)}) async-start(), calls=%async_computation.9 | async-start | bytes 5242880 | tf_op jit(solution)/shard_map/reduce_scatter | solution.py:83
  117.6 0.7 copy-start
  117.6 333.3 %all-gather.7.cloned.1.call-start = ((), (), s32[]{:S(2)}) async-start(), calls=%async_computation.6 | async-start | bytes 2621440 | tf_op jit(solution)/shard_map/all_gather | solution.py:71
  323.9 1.5 copy-start.1
  325.4 239.0 %all-gather.11.cloned.1.call-start = ((), (), s32[]{:S(2)}) async-start(), calls=%async_computation.10 | async-start | bytes 7864320 | tf_op jit(solution)/shard_map/all_gather | solution.py:97
  417.5 248.6 %reduce-scatter.7.cloned.1.call-start = ((), (), s32[]{:S(2)}) async-start(), calls=%async_computation.7 | async-start | bytes 7077888 | tf_op jit(solution)/shard_map/reduce_scatter | solution.py:75
  462.3 232.1 %reduce-scatter.11.cloned.1.call-start = ((), (), s32[]{:S(2)}) async-start(), calls=%async_computation.11 | async-start | bytes 7077888 | tf_op jit(solution)/shard_map/reduce_scatter | solution.py:105
  590.6 12.6 %slice-start = ((s8[6291456]{0:T(1024)(128)(4,1)}), s8[2097152]{0:T(1024)(128)(4,1)S(1)}, s32[]{:S(2)}) async-start(s8[6291456]{0:T(1024)(128)(4,1)} %bitcast.74), calls=%async_computation.12 | async-start | bytes 4194304
  590.6 12.6 %slice-start.1 = ((s8[6291456]{0:T(1024)(128)(4,1)}), s8[4194304]{0:T(1024)(128)(4,1)S(1)}, s32[]{:S(2)}) async-start(s8[6291456]{0:T(1024)(128)(4,1)} %bitcast.74), calls=%async_computation.13 | async-start | bytes 8388608
Sparse Core Ops, SparseCore 0:
  9.9 48.2 all-gather.4
  60.0 45.5 all-gather.8
  108.5 211.8 reduce-scatter.4
  322.5 77.8 reduce-scatter.8
  402.4 48.4 all-gather.6
  453.0 111.3 all-gather.10
  568.7 59.9 reduce-scatter.6
  632.6 61.7 reduce-scatter.10
where the time goes:
time: 703 us; the launch traced here: 701 us
  waiting for transfers between devices  488 us (69%)
  matrix products  130 us (18%)
  local copies, waits for them, and re-layouts  64.9 us (9%)
  between operations  14.2 us (2%)
    reduce_scatter x1, waiting for transfers between devices, per_device(): lax.psum_scatter(jnp.dot(piece, qkv_flat, preferred_element_type=jnp.floa...  202 us
    all_gather x1, waiting for transfers between devices, per_device(): lax.all_gather(d_projected.reshape(seq_len, local_heads * 3 * head_size),...  102 us
    reduce_scatter x1, waiting for transfers between devices, per_device(): lax.psum_scatter(lax.dot_general(piece, out_flat, contract_last, preferre...  74.8 us
    unnamed x10, local copies, waits for them, and re-layouts  62.8 us
    all_gather x2, waiting for transfers between devices, gather_rows(): gathered = lax.all_gather(local_rows, ('row', 'col'), axis=0, tiled=True)  46.1 us
    all_gather x1, waiting for transfers between devices, per_device(): lax.all_gather(mixed_heads.reshape(seq_len, local_heads * head_size), 'de...  33.4 us
    reduce_scatter x1, waiting for transfers between devices, per_device(): lax.psum_scatter(lax.dot_general(piece, qkv_flat, contract_last, preferre...  28.3 us
    dot_general x1, matrix products, per_device(): jnp.dot(piece, qkv_flat, preferred_element_type=jnp.float32)  26.2 us
  transfers between devices with their start and end apart: 8, of which 7 were waited for; matrix products, arithmetic and copies ran while one was open for 28% of the time, Pallas kernels for 0%

commit v1 on v0

v1 whole, which is shorter than its diff:
```python
import functools
import math

import jax
import jax.numpy as jnp
from jax import lax
from jax.experimental import pallas as pl
from jax.experimental.pallas import tpu as pltpu
from jax.sharding import PartitionSpec as P

PIECES = 2
VMEM_LIMIT = 56 * 1024 * 1024
CONTRACT_FIRST = (((0,), (0,)), ((), ()))
CONTRACT_LAST = (((1,), (1,)), ((), ()))


def dot_f32(left, right, dims=(((1,), (0,)), ((), ()))):
    return lax.dot_general(left, right, dims, preferred_element_type=jnp.float32)


def softmax_rows(positions, queries, key_rows, score_scale):
    seq_len = queries.shape[0]
    scores = dot_f32(queries, key_rows, CONTRACT_LAST) * score_scale
    rows = lax.broadcasted_iota(jnp.int32, (seq_len, seq_len), 0)
    cols = lax.broadcasted_iota(jnp.int32, (seq_len, seq_len), 1)
    allowed = (cols <= rows) & (cols >= rows - positions)
    weights = jnp.where(allowed, jnp.exp(scores), 0.0)
    return weights / jnp.sum(weights, axis=-1, keepdims=True)


def attend_kernel(score_scale, head, positions_ref, projected_ref, mixed_ref):
    queries = projected_ref[:, :head]
    key_rows = projected_ref[:, head : 2 * head]
    value_rows = projected_ref[:, 2 * head :]
    probabilities = softmax_rows(positions_ref[...], queries, key_rows, score_scale)
    mixed_ref[...] = dot_f32(probabilities.astype(jnp.bfloat16), value_rows).astype(jnp.bfloat16)


def attend_back_kernel(score_scale, head, positions_ref, projected_ref, d_mixed_ref, grads_ref):
    queries = projected_ref[:, :head]
    key_rows = projected_ref[:, head : 2 * head]
    value_rows = projected_ref[:, 2 * head :]
    d_mixed = d_mixed_ref[...]
    probabilities = softmax_rows(positions_ref[...], queries, key_rows, score_scale)
    rounded = probabilities.astype(jnp.bfloat16)
    d_probs = dot_f32(d_mixed, value_rows, CONTRACT_LAST)
    row_delta = jnp.sum(probabilities * d_probs, axis=-1, keepdims=True)
    d_scores = (probabilities * (d_probs - row_delta) * score_scale).astype(jnp.bfloat16)
    grads_ref[:, :head] = dot_f32(d_scores, key_rows).astype(jnp.bfloat16)
    grads_ref[:, head : 2 * head] = dot_f32(d_scores, queries, CONTRACT_FIRST).astype(jnp.bfloat16)
    grads_ref[:, 2 * head :] = dot_f32(rounded, d_mixed, CONTRACT_FIRST).astype(jnp.bfloat16)


def attention_call(kernel, positions, head, heads, wide_out, *arrays):
    seq_len = positions.shape[0]
    score_scale = 1.0 / math.sqrt(head)

    def per_head(width):
        return pl.BlockSpec((seq_len, width), lambda h: (0, h))

    out_width = 3 * head if wide_out else head
    flops = (14 if wide_out else 4) * heads * seq_len * seq_len * head
    return pl.pallas_call(
        functools.partial(kernel, score_scale, head),
        grid=(heads,),
        in_specs=[pl.BlockSpec((seq_len, 1), lambda h: (0, 0))]
        + [per_head(a.shape[1] // heads) for a in arrays],
        out_specs=per_head(out_width),
        out_shape=jax.ShapeDtypeStruct((seq_len, heads * out_width), jnp.bfloat16),
        cost_estimate=pl.CostEstimate(
            flops=flops,
            bytes_accessed=8 * seq_len * heads * out_width,
            transcendentals=heads * seq_len * seq_len,
        ),
        compiler_params=pltpu.CompilerParams(vmem_limit_bytes=VMEM_LIMIT),
    )(positions.reshape(seq_len, 1), *arrays)


def qkv_weight_kernel(heads, head, tokens_ref, grads_ref, out_ref):
    block = tokens_ref.shape[1]
    left = tokens_ref[...].T
    for pair in range(heads * 3 // 2):
        term = dot_f32(left, grads_ref[:, 2 * pair * head : (2 * pair + 2) * head])
        for half in range(2):
            at_head, part = divmod(2 * pair + half, 3)
            out_ref[pl.ds(part * heads + at_head, block, stride=3 * heads), :] = term[
                :, half * head : (half + 1) * head
            ]


def qkv_weight_grad(tokens_all, grads_all, heads, head):
    count, width = tokens_all.shape
    columns = grads_all.shape[1]
    block = 256
    rows = pl.pallas_call(
        functools.partial(qkv_weight_kernel, heads, head),
        grid=(width // block,),
        in_specs=[
            pl.BlockSpec((count, block), lambda i: (0, i)),
            pl.BlockSpec((count, columns), lambda i: (0, 0)),
        ],
        out_specs=pl.BlockSpec((block * 3 * heads, head), lambda i: (i, 0)),
        out_shape=jax.ShapeDtypeStruct((width * 3 * heads, head), jnp.float32),
        cost_estimate=pl.CostEstimate(
            flops=2 * count * width * columns,
            bytes_accessed=4 * width * columns + 2 * count * (width + columns),
            transcendentals=0,
        ),
        compiler_params=pltpu.CompilerParams(vmem_limit_bytes=VMEM_LIMIT),
    )(tokens_all, grads_all)
    return rows.reshape(width, 3, heads, head).transpose(0, 2, 1, 3)


def send_on(block, size):
    return lax.ppermute(block, "depth", [(i, (i + 1) % size) for i in range(size)])


def ring_sum(partial, size):
    me = lax.axis_index("depth")

    def chunk(back):
        return lax.dynamic_index_in_dim(partial, lax.rem(me + 2 * size - back, size), 0, False)

    running = chunk(1).astype(jnp.bfloat16)
    for step in range(1, size):
        arrived = send_on(running, size).astype(jnp.float32)
        running = (arrived + chunk(1 + step)).astype(jnp.bfloat16)
    return running


def ring_gather(block, size):
    me = lax.axis_index("depth")
    out = jnp.zeros((size,) + block.shape, block.dtype)
    out = lax.dynamic_update_index_in_dim(out, block, me, 0)
    for step in range(1, size):
        block = send_on(block, size)
        out = lax.dynamic_update_index_in_dim(out, block, lax.rem(me + size - step, size), 0)
    return out


def gather_rows(local_rows):
    return lax.all_gather(local_rows, ("row", "col"), axis=0, tiled=True)


def scatter_rows(whole):
    return lax.psum_scatter(whole, ("row", "col"), scatter_dimension=0, tiled=True)


def per_device(size, tokens, w_qkv, w_out, positions, d_output):
    seq_len = positions.shape[0]
    width, heads, _, head = w_qkv.shape
    hidden = heads * head
    columns = 3 * hidden
    local_rows = tokens.shape[0]
    part_rows = local_rows // PIECES
    sharers = seq_len // local_rows
    qkv_flat = w_qkv.reshape(width, columns)
    out_flat = w_out.reshape(hidden, width)

    gathered = [
        gather_rows(tokens[p * part_rows : (p + 1) * part_rows]) for p in range(PIECES)
    ]
    pieces = []
    for piece in gathered:
        partial = dot_f32(piece, qkv_flat)
        pieces.append(ring_sum(partial.reshape(size, sharers * part_rows, columns), size))
    projected = jnp.stack([p.reshape(sharers, part_rows, columns) for p in pieces], axis=1)
    projected = projected.reshape(seq_len, columns)

    grad_all = gather_rows(d_output)
    d_mixed = dot_f32(grad_all, out_flat, CONTRACT_LAST)
    d_mixed = ring_sum(d_mixed.reshape(size, seq_len, hidden), size)

    mixed = attention_call(attend_kernel, positions, head, heads, False, projected)
    heads_all = ring_gather(mixed, size).reshape(size * seq_len, hidden)
    output = scatter_rows(dot_f32(heads_all, out_flat).astype(jnp.bfloat16))

    grads = attention_call(
        attend_back_kernel, positions, head, heads, True, projected, d_mixed
    )
    d_out_weight = dot_f32(heads_all, grad_all, CONTRACT_FIRST)

    grads = grads.reshape(sharers, PIECES, part_rows, columns)
    all_grads = []
    d_tokens = []
    for p in range(PIECES):
        piece = ring_gather(grads[:, p].reshape(sharers * part_rows, columns), size)
        piece = piece.reshape(size * sharers * part_rows, columns)
        all_grads.append(piece)
        d_tokens.append(
            scatter_rows(dot_f32(piece, qkv_flat, CONTRACT_LAST).astype(jnp.bfloat16))
        )
    d_qkv_weight = qkv_weight_grad(
        jnp.concatenate(gathered, axis=0), jnp.concatenate(all_grads, axis=0), heads, head
    )
    return (
        output,
        jnp.concatenate(d_tokens, axis=0),
        d_qkv_weight,
        d_out_weight.reshape(heads, head, width),
    )


def solution(mesh):
    return jax.shard_map(
        functools.partial(per_device, mesh.shape["depth"]),
        mesh=mesh,
        in_specs=(
            P(("row", "col"), "depth"),
            P("depth", ("row", "col"), None, None),
            P(("row", "col"), None, "depth"),
            P("depth"),
            P(("row", "col"), "depth"),
        ),
        out_specs=(
            P(("row", "col"), "depth"),
            P(("row", "col"), "depth"),
            P("depth", ("row", "col"), None, None),
            P(("row", "col"), None, "depth"),
        ),
        check_vma=False,
    )
```

time: 703 us -> 508 us (0.72)
  waiting for transfers between devices: 488 us -> 269 us
  Pallas kernels: 0 us -> 45.9 us
  matrix products: 130 us -> 94.8 us
  other arithmetic: 3.62 us -> 23.7 us
  local copies, waits for them, and re-layouts: 64.9 us -> 52.1 us
    reduce_scatter x4 -> x3, waiting for transfers between devices: 305 us -> 21.2 us  [scatter_rows(): lax.psum_scatter(whole, ('row', 'col'), scatter_dimension=0, tiled=True)]
    ppermute x0 -> x18, waiting for transfers between devices: none -> 220 us  [send_on(): lax.ppermute(block, 'depth', [(i, (i + 1) % size) for i in range(size)])]
    all_gather x4 -> x3, waiting for transfers between devices: 181 us -> 26.6 us  [gather_rows(): return lax.all_gather(local_rows, ('row', 'col'), axis=0, tiled=True)]
    pallas_call x0 -> x3, Pallas kernels: none -> 45.9 us  [the longest x1 30.5 us: qkv_weight_grad(): pl.pallas_call(functools.partial(qkv_weight_kernel, heads, head), grid=(w...]
    dot_general x12 -> x7, matrix products: 130 us -> 94.8 us  [dot_f32(): lax.dot_general(left, right, dims, preferred_element_type=jnp.float32)]
    unnamed x10 -> x17, local copies, waits for them, and re-layouts: 62.8 us -> 31.1 us
    concatenate x0 -> x3, other arithmetic: none -> 11.1 us  [the longest x1 5.95 us: per_device(): jnp.concatenate(gathered, axis=0)]
    dynamic_update_slice x0 -> x12, local copies, waits for them, and re-layouts: none -> 10.4 us  [the longest x9 6.84 us: ring_gather(): lax.dynamic_update_index_in_dim(out, block, lax.rem(me + size - step, siz...]
  transfers between devices with their start and end apart: 8 -> 24, of which waited for: 7 -> 17; matrix products, arithmetic and copies ran while one was open for 28% -> 31% of each run, Pallas kernels for 0% -> 7%
where the time goes in v1:
time: 508 us; the launch traced here: 507 us
  waiting for transfers between devices  269 us (53%)
  matrix products  94.8 us (19%)
  local copies, waits for them, and re-layouts  52.1 us (10%)
  Pallas kernels  45.9 us (9%)
  other arithmetic  23.7 us (5%)
  between operations  14.4 us (3%)
  starting transfers between devices  6.44 us (1%)
    ppermute x18, waiting for transfers between devices, send_on(): lax.ppermute(block, 'depth', [(i, (i + 1) % size) for i in range(size)])  220 us
    dot_general x7, matrix products, dot_f32(): lax.dot_general(left, right, dims, preferred_element_type=jnp.float32)  94.8 us
    unnamed x17, local copies, waits for them, and re-layouts  31.1 us
    pallas_call x1, Pallas kernels, qkv_weight_grad(): pl.pallas_call(functools.partial(qkv_weight_kernel, heads, head), grid=(w...  30.5 us
    all_gather x3, waiting for transfers between devices, gather_rows(): return lax.all_gather(local_rows, ('row', 'col'), axis=0, tiled=True)  26.6 us
    reduce_scatter x3, waiting for transfers between devices, scatter_rows(): lax.psum_scatter(whole, ('row', 'col'), scatter_dimension=0, tiled=True)  21.2 us
    pallas_call x2, Pallas kernels, attention_call(): pl.pallas_call(functools.partial(kernel, score_scale, head), grid=(heads,...  15.4 us
    convert_element_type x9, other arithmetic, ring_sum(): running = (arrived + chunk(1 + step)).astype(jnp.bfloat16)  11.3 us
  transfers between devices with their start and end apart: 24, of which 17 were waited for; matrix products, arithmetic and copies ran while one was open for 31% of the time, Pallas kernels for 7%

profile of v1, /device:TPU:0, one launch (start us, length us, event | category | flops | bytes accessed | tf_op | source)
XLA Modules:
  0.0 506.6 jit_solution(15109683774863309698)
XLA Ops:
  10.8 24.5 %copy.11 = bf16[3072,8,3,128]{0,3,2,1:T(8,128)(2,1)} copy(bf16[3072,8,3,128]{3,1,2,0:T(8,128)(2,1)} %param.6) | data formatting | bytes 37748736 | tf_op args[1]
  35.3 10.2 %all-gather.6.cloned.1.call-done = bf16[512,3072]{1,0:T(8,128)(2,1)} async-done(((bf16[64,3072]{1,0:T(8,128)(2,1)}), bf16[512,3072]{1,0:T(8,128)(2,1)}) %all-gather.6.cloned.1.call-update) | async-done | bytes 3145744 | tf_op jit(solution)/shard_map/all_gather | solution.py:142
  45.5 14.1 %fusion.17 = f32[4,128,3072]{2,1,0:T(8,128)S(1)} fusion(bf16[4,128,3072]{2,1,0:T(8,128)(2,1)} %bitcast.125, bf16[3072,3072,1]{0,1,2:T(8,128)(2,1)} %bitcast.110), kind=kOutput, calls=%fused_computation.48 | convolution fusion | flops 9663676416 | bytes 28311552 | tf_op jit(solution)/shard_map/dot_general | solution.py:18
  59.6 2.7 copy-done.4
  63.9 16.4 %all-gather.4.cloned.1.call-done = bf16[512,3072]{1,0:T(8,128)(2,1)} async-done(((bf16[64,3072]{1,0:T(8,128)(2,1)}), bf16[512,3072]{1,0:T(8,128)(2,1)}) %all-gather.4.cloned.1.call-update) | async-done | bytes 3145744 | tf_op jit(solution)/shard_map/all_gather | solution.py:142
  80.3 14.1 %fusion.16 = f32[4,128,3072]{2,1,0:T(8,128)S(1)} fusion(bf16[4,128,3072]{2,1,0:T(8,128)(2,1)} %bitcast.126, bf16[3072,3072,1]{0,1,2:T(8,128)(2,1)} %bitcast.111), kind=kOutput, calls=%fused_computation.47 | convolution fusion | flops 9663676416 | bytes 28311552 | tf_op jit(solution)/shard_map/dot_general | solution.py:18
  102.8 16.6 %collective-permute-done = bf16[128,3072]{1,0:T(8,128)(2,1)S(1)} collective-permute-done((bf16[128,3072]{1,0:T(8,128)(2,1)S(1)}, bf16[128,3072]{1,0:T(8,128)(2,1)S(1)}, u32[]{:S(2)}, u32[]{:S(2)}) %collective-permute-start) | collective-permute-done | bytes 786464 | tf_op jit(solution)/shard_map/ppermute | solution.py:115
  121.8 14.5 %collective-permute-done.4 = bf16[128,3072]{1,0:T(8,128)(2,1)} collective-permute-done((bf16[128,3072]{1,0:T(8,128)(2,1)S(1)}, bf16[128,3072]{1,0:T(8,128)(2,1)}, u32[]{:S(2)}, u32[]{:S(2)}) %collective-permute-start.4) | collective-permute-done | bytes 786464 | tf_op jit(solution)/shard_map/ppermute | solution.py:115
  136.3 2.8 fusion.3
  139.1 10.8 %fusion.18 = f32[4,256,1024]{2,1,0:T(8,128)S(1)} fusion(bf16[4,256,3072]{2,1,0:T(8,128)(2,1)} %bitcast.133, bf16[1024,3072,1]{1,0,2:T(8,128)(2,1)} %bitcast.131), kind=kOutput, calls=%fused_computation.49 | convolution fusion | flops 6442450944 | bytes 16777216 | tf_op jit(solution)/shard_map/dot_general | solution.py:18
  154.5 26.6 %collective-permute-done.9 = bf16[256,1024]{1,0:T(8,128)(2,1)S(1)} collective-permute-done((bf16[256,1024]{1,0:T(8,128)(2,1)S(1)}, bf16[256,1024]{1,0:T(8,128)(2,1)S(1)}, u32[]{:S(2)}, u32[]{:S(2)}) %collective-permute-start.9) | collective-permute-done | bytes 524320 | tf_op jit(solution)/shard_map/ppermute | solution.py:115
  183.1 25.4 %collective-permute-done.10 = bf16[256,1024]{1,0:T(8,128)(2,1)S(1)} collective-permute-done((bf16[256,1024]{1,0:T(8,128)(2,1)S(1)}, bf16[256,1024]{1,0:T(8,128)(2,1)S(1)}, u32[]{:S(2)}, u32[]{:S(2)}) %collective-permute-start.10) | collective-permute-done | bytes 524320 | tf_op jit(solution)/shard_map/ppermute | solution.py:115
  210.3 13.6 %collective-permute-done.11 = bf16[256,1024]{1,0:T(8,128)(2,1)S(1)} collective-permute-done((bf16[256,1024]{1,0:T(8,128)(2,1)S(1)}, bf16[256,1024]{1,0:T(8,128)(2,1)S(1)}, u32[]{:S(2)}, u32[]{:S(2)}) %collective-permute-start.11) | collective-permute-done | bytes 524320 | tf_op jit(solution)/shard_map/ppermute | solution.py:115
  224.8 8.3 %shard_map.85 = bf16[256,3072]{1,0:T(8,128)(2,1)} custom-call(s32[256,1]{1,0:T(8,128)} %copy.16.positions_ref, bf16[256,3072]{1,0:T(8,128)(2,1)} %bitcast.114, bf16[256,1024]{1,0:T(8,128)(2,1)} %fusion.8.d_mixed_ref), custom_call_target="tpu_custom_call" | custom-call | flops 939524096 | bytes 6291456 | tf_op jit(solution)/shard_map/pallas_call | solution.py:63
  237.3 21.0 %collective-permute-done.15 = bf16[128,3072]{1,0:T(8,128)(2,1)} collective-permute-done((bf16[128,3072]{1,0:T(8,128)(2,1)}, bf16[128,3072]{1,0:T(8,128)(2,1)}, u32[]{:S(2)}, u32[]{:S(2)}) %collective-permute-start.15) | collective-permute-done | bytes 786464 | tf_op jit(solution)/shard_map/ppermute | solution.py:115
  259.9 15.3 %collective-permute-done.12 = bf16[128,3072]{1,0:T(8,128)(2,1)} collective-permute-done((bf16[128,3072]{1,0:T(8,128)(2,1)}, bf16[128,3072]{1,0:T(8,128)(2,1)}, u32[]{:S(2)}, u32[]{:S(2)}) %collective-permute-start.12) | collective-permute-done | bytes 786464 | tf_op jit(solution)/shard_map/ppermute | solution.py:115
  276.4 15.5 %collective-permute-done.16 = bf16[128,3072]{1,0:T(8,128)(2,1)S(1)} collective-permute-done((bf16[128,3072]{1,0:T(8,128)(2,1)}, bf16[128,3072]{1,0:T(8,128)(2,1)S(1)}, u32[]{:S(2)}, u32[]{:S(2)}) %collective-permute-start.16) | collective-permute-done | bytes 786464 | tf_op jit(solution)/shard_map/ppermute | solution.py:115
  293.2 15.7 %collective-permute-done.13 = bf16[128,3072]{1,0:T(8,128)(2,1)} collective-permute-done((bf16[128,3072]{1,0:T(8,128)(2,1)}, bf16[128,3072]{1,0:T(8,128)(2,1)}, u32[]{:S(2)}, u32[]{:S(2)}) %collective-permute-start.13) | collective-permute-done | bytes 786464 | tf_op jit(solution)/shard_map/ppermute | solution.py:115
  309.0 16.7 %collective-permute-done.17 = bf16[128,3072]{1,0:T(8,128)(2,1)S(1)} collective-permute-done((bf16[128,3072]{1,0:T(8,128)(2,1)S(1)}, bf16[128,3072]{1,0:T(8,128)(2,1)S(1)}, u32[]{:S(2)}, u32[]{:S(2)}) %collective-permute-start.17) | collective-permute-done | bytes 786464 | tf_op jit(solution)/shard_map/ppermute | solution.py:115
  325.7 15.0 %convolution_convert_fusion.1 = bf16[512,3072]{1,0:T(8,128)(2,1)} fusion(bf16[512,3072]{1,0:T(8,128)(2,1)S(1)} %bitcast.116, bf16[3072,3072]{0,1:T(8,128)(2,1)} %bitcast.112), kind=kOutput, calls=%fused_computation.5 | convolution fusion | flops 9665249280 | bytes 25165824 | tf_op jit(solution)/shard_map/dot_general | solution.py:18
  345.0 16.8 %convolution_convert_fusion.2 = bf16[512,3072]{1,0:T(8,128)(2,1)} fusion(bf16[512,3072]{1,0:T(8,128)(2,1)} %bitcast.118, bf16[3072,3072]{0,1:T(8,128)(2,1)} %bitcast.113), kind=kOutput, calls=%fused_computation.6 | convolution fusion | flops 9665249280 | bytes 25165824 | tf_op jit(solution)/shard_map/dot_general | solution.py:18
  361.9 7.1 %shard_map.84 = bf16[256,1024]{1,0:T(8,128)(2,1)} custom-call(s32[256,1]{1,0:T(8,128)} %copy.16.positions_ref, bf16[256,3072]{1,0:T(8,128)(2,1)} %bitcast.115), custom_call_target="tpu_custom_call" | custom-call | flops 268435456 | bytes 2097152 | tf_op jit(solution)/shard_map/pallas_call | solution.py:63
  368.9 13.5 %collective-permute-done.6 = bf16[256,1024]{1,0:T(8,128)(2,1)S(1)} collective-permute-done((bf16[256,1024]{1,0:T(8,128)(2,1)}, bf16[256,1024]{1,0:T(8,128)(2,1)S(1)}, u32[]{:S(2)}, u32[]{:S(2)}) %collective-permute-start.6) | collective-permute-done | bytes 524320 | tf_op jit(solution)/shard_map/ppermute | solution.py:115
  382.4 14.3 %collective-permute-done.7 = bf16[256,1024]{1,0:T(8,128)(2,1)S(1)} collective-permute-done((bf16[256,1024]{1,0:T(8,128)(2,1)S(1)}, bf16[256,1024]{1,0:T(8,128)(2,1)S(1)}, u32[]{:S(2)}, u32[]{:S(2)}) %collective-permute-start.7) | collective-permute-done | bytes 524320 | tf_op jit(solution)/shard_map/ppermute | solution.py:115
  398.2 9.5 %collective-permute-done.8 = bf16[256,1024]{1,0:T(8,128)(2,1)S(1)} collective-permute-done((bf16[256,1024]{1,0:T(8,128)(2,1)S(1)}, bf16[256,1024]{1,0:T(8,128)(2,1)S(1)}, u32[]{:S(2)}, u32[]{:S(2)}) %collective-permute-start.8) | collective-permute-done | bytes 524320 | tf_op jit(solution)/shard_map/ppermute | solution.py:115
  409.1 11.7 %convolution_convert_fusion = bf16[1024,3072]{1,0:T(8,128)(2,1)} fusion(bf16[1024,1024]{1,0:T(8,128)(2,1)S(1)} %bitcast.120, bf16[1024,3072]{1,0:T(8,128)(2,1)} %bitcast.132), kind=kOutput, calls=%fused_computation.4 | convolution fusion | flops 6445596672 | bytes 14680064 | tf_op jit(solution)/shard_map/dot_general | solution.py:18
  420.8 5.9 %pad_maximum_fusion.tokens_ref = bf16[1024,3072]{1,0:T(8,128)(2,1)} fusion(bf16[512,3072]{1,0:T(8,128)(2,1)} %all-gather.6.cloned.1.call-done, bf16[512,3072]{1,0:T(8,128)(2,1)} %all-gather.4.cloned.1.call-done), kind=kLoop, calls=%fused_computation | loop fusion | flops 12582912 | bytes 12582912 | tf_op jit(solution)/shard_map/concatenate | solution.py:194
  426.7 3.9 copy.23
  430.7 12.3 %fusion = f32[8,128,3072]{2,1,0:T(8,128)} fusion(bf16[8,128,1024]{2,1,0:T(8,128)(2,1)} %bitcast.129, bf16[1024,3072]{1,0:T(8,128)(2,1)} %all-gather.8.cloned.1.call-done), kind=kOutput, calls=%fused_computation.2 | convolution fusion | flops 6442450944 | bytes 20971520 | tf_op jit(solution)/shard_map/dot_general | solution.py:18
  443.0 3.1 pad_maximum_fusion.1.grads_ref
  446.0 30.5 %shard_map.86 = f32[73728,128]{1,0:T(8,128)} custom-call(bf16[1024,3072]{1,0:T(8,128)(2,1)} %pad_maximum_fusion.tokens_ref, bf16[1024,3072]{1,0:T(8,128)(2,1)} %pad_maximum_fusion.1.grads_ref), custom_call_target="tpu_custom_call" | custom-call | flops 19327352832 | bytes 50331648 | tf_op jit(solution)/shard_map/pallas_call | solution.py:95
  478.6 21.2 %reduce-scatter.4.cloned.1.call-done = bf16[128,3072]{1,0:T(8,128)(2,1)} async-done(((bf16[1024,3072]{1,0:T(8,128)(2,1)}), bf16[128,3072]{1,0:T(8,128)(2,1)}) %reduce-scatter.4.cloned.1.call-update) | async-done | bytes 786448 | tf_op jit(solution)/shard_map/reduce_scatter | solution.py:146
  (85 shorter events, 42.7 us)
Async XLA Ops:
  7.2 38.3 %all-gather.6.cloned.1.call-start = ((), (), s32[]{:S(2)}) async-start(), calls=%async_computation.4 | async-start | bytes 3538944 | tf_op jit(solution)/shard_map/all_gather | solution.py:142
  9.3 71.0 %all-gather.4.cloned.1.call-start = ((), (), s32[]{:S(2)}) async-start(), calls=%async_computation.3 | async-start | bytes 3538944 | tf_op jit(solution)/shard_map/all_gather | solution.py:142
  10.0 129.1 %all-gather.8.cloned.1.call-start = ((), (), s32[]{:S(2)}) async-start(), calls=%async_computation.6 | async-start | bytes 7077888 | tf_op jit(solution)/shard_map/all_gather | solution.py:142
  10.8 465.8 %reduce-scatter.8.cloned.1.call-start = ((), (), s32[]{:S(2)}) async-start(), calls=%async_computation.8 | async-start | bytes 3538944 | tf_op jit(solution)/shard_map/reduce_scatter | solution.py:146
  59.6 2.7 copy-start.4
  62.4 36.3 %collective-permute-start.3 = (bf16[128,3072]{1,0:T(8,128)(2,1)S(1)}, bf16[128,3072]{1,0:T(8,128)(2,1)}, u32[]{:S(2)}, u32[]{:S(2)}) collective-permute-start(bf16[128,3072]{1,0:T(8,128)(2,1)S(1)} %fusion.12), channel_id=1, source_target_pairs={{0,1},{1,2},{2,3},{3,0},{4,5},{5,6},{6,7},{7,4},{8,9},{9,10},{10,1... | collective-permute-start | bytes 2359304 | tf_op jit(solution)/shard_map/ppermute | solution.py:115
  94.4 2.6 copy-start.3
  97.0 5.0 copy-start.5
  97.1 22.2 %collective-permute-start = (bf16[128,3072]{1,0:T(8,128)(2,1)S(1)}, bf16[128,3072]{1,0:T(8,128)(2,1)S(1)}, u32[]{:S(2)}, u32[]{:S(2)}) collective-permute-start(bf16[128,3072]{1,0:T(8,128)(2,1)S(1)} %fusion.11), channel_id=1, source_target_pairs={{0,1},{1,2},{2,3},{3,0},{4,5},{5,6},{6,7},{7,4},{8,9},{9,10},{10,1... | collective-permute-start | bytes 2359304 | tf_op jit(solution)/shard_map/ppermute | solution.py:115
  100.4 35.9 %collective-permute-start.4 = (bf16[128,3072]{1,0:T(8,128)(2,1)S(1)}, bf16[128,3072]{1,0:T(8,128)(2,1)}, u32[]{:S(2)}, u32[]{:S(2)}) collective-permute-start(bf16[128,3072]{1,0:T(8,128)(2,1)S(1)} %fusion.4), channel_id=1, source_target_pairs={{0,1},{1,2},{2,3},{3,0},{4,5},{5,6},{6,7},{7,4},{8,9},{9,10},{10,1... | collective-permute-start | bytes 2359304 | tf_op jit(solution)/shard_map/ppermute | solution.py:115
  121.8 31.4 %collective-permute-start.1 = (bf16[128,3072]{1,0:T(8,128)(2,1)}, bf16[128,3072]{1,0:T(8,128)(2,1)}, u32[]{:S(2)}, u32[]{:S(2)}) collective-permute-start(bf16[128,3072]{1,0:T(8,128)(2,1)} %fusion.7), channel_id=1, source_target_pairs={{0,1},{1,2},{2,3},{3,0},{4,5},{5,6},{6,7},{7,4},{8,9},{9,10},{10,1... | collective-permute-start | bytes 2359304 | tf_op jit(solution)/shard_map/ppermute | solution.py:115
  136.3 16.9 %slice-start = ((s8[6291456]{0:T(1024)(128)(4,1)}), s8[2097152]{0:T(1024)(128)(4,1)S(1)}, s32[]{:S(2)}) async-start(s8[6291456]{0:T(1024)(128)(4,1)} %bitcast.123), calls=%async_computation.9 | async-start | bytes 4194304
  139.1 42.5 %collective-permute-start.5 = (bf16[128,3072]{1,0:T(8,128)(2,1)}, bf16[128,3072]{1,0:T(8,128)(2,1)S(1)}, u32[]{:S(2)}, u32[]{:S(2)}) collective-permute-start(bf16[128,3072]{1,0:T(8,128)(2,1)} %fusion.3), channel_id=1, source_target_pairs={{0,1},{1,2},{2,3},{3,0},{4,5},{5,6},{6,7},{7,4},{8,9},{9,10},{10,1... | collective-permute-start | bytes 2359304 | tf_op jit(solution)/shard_map/ppermute | solution.py:115
  139.1 14.1 %slice-start.1 = ((s8[6291456]{0:T(1024)(128)(4,1)}), s8[4194304]{0:T(1024)(128)(4,1)S(1)}, s32[]{:S(2)}) async-start(s8[6291456]{0:T(1024)(128)(4,1)} %bitcast.123), calls=%async_computation.10 | async-start | bytes 8388608
  150.0 31.1 %collective-permute-start.9 = (bf16[256,1024]{1,0:T(8,128)(2,1)S(1)}, bf16[256,1024]{1,0:T(8,128)(2,1)S(1)}, u32[]{:S(2)}, u32[]{:S(2)}) collective-permute-start(bf16[256,1024]{1,0:T(8,128)(2,1)S(1)} %fusion.13), channel_id=1, source_target_pairs={{0,1},{1,2},{2,3},{3,0},{4,5},{5,6},{6,7},{7,4},{8,9},{9,10},{10,1... | collective-permute-start | bytes 1572872 | tf_op jit(solution)/shard_map/ppermute | solution.py:115
  154.5 54.4 %collective-permute-start.2 = (bf16[128,3072]{1,0:T(8,128)(2,1)S(1)}, bf16[128,3072]{1,0:T(8,128)(2,1)S(1)}, u32[]{:S(2)}, u32[]{:S(2)}) collective-permute-start(bf16[128,3072]{1,0:T(8,128)(2,1)S(1)} %fusion.6), channel_id=1, source_target_pairs={{0,1},{1,2},{2,3},{3,0},{4,5},{5,6},{6,7},{7,4},{8,9},{9,10},{10,1... | collective-permute-start | bytes 2359304 | tf_op jit(solution)/shard_map/ppermute | solution.py:115
  181.3 27.3 %collective-permute-start.10 = (bf16[256,1024]{1,0:T(8,128)(2,1)S(1)}, bf16[256,1024]{1,0:T(8,128)(2,1)S(1)}, u32[]{:S(2)}, u32[]{:S(2)}) collective-permute-start(bf16[256,1024]{1,0:T(8,128)(2,1)S(1)} %fusion.10), channel_id=1, source_target_pairs={{0,1},{1,2},{2,3},{3,0},{4,5},{5,6},{6,7},{7,4},{8,9},{9,10},{10,1... | collective-permute-start | bytes 1572872 | tf_op jit(solution)/shard_map/ppermute | solution.py:115
  208.7 15.1 %collective-permute-start.11 = (bf16[256,1024]{1,0:T(8,128)(2,1)S(1)}, bf16[256,1024]{1,0:T(8,128)(2,1)S(1)}, u32[]{:S(2)}, u32[]{:S(2)}) collective-permute-start(bf16[256,1024]{1,0:T(8,128)(2,1)S(1)} %fusion.9), channel_id=1, source_target_pairs={{0,1},{1,2},{2,3},{3,0},{4,5},{5,6},{6,7},{7,4},{8,9},{9,10},{10,1... | collective-permute-start | bytes 1572872 | tf_op jit(solution)/shard_map/ppermute | solution.py:115
  235.7 22.6 %collective-permute-start.15 = (bf16[128,3072]{1,0:T(8,128)(2,1)}, bf16[128,3072]{1,0:T(8,128)(2,1)}, u32[]{:S(2)}, u32[]{:S(2)}) collective-permute-start(bf16[128,3072]{1,0:T(8,128)(2,1)} %bitcast.39), channel_id=1, source_target_pairs={{0,1},{1,2},{2,3},{3,0},{4,5},{5,6},{6,7},{7,4},{8,9},{9,10},{10,1... | collective-permute-start | bytes 2359304 | tf_op jit(solution)/shard_map/ppermute | solution.py:115
  235.7 39.4 %collective-permute-start.12 = (bf16[128,3072]{1,0:T(8,128)(2,1)}, bf16[128,3072]{1,0:T(8,128)(2,1)}, u32[]{:S(2)}, u32[]{:S(2)}) collective-permute-start(bf16[128,3072]{1,0:T(8,128)(2,1)} %bitcast.33), channel_id=1, source_target_pairs={{0,1},{1,2},{2,3},{3,0},{4,5},{5,6},{6,7},{7,4},{8,9},{9,10},{10,1... | collective-permute-start | bytes 2359304 | tf_op jit(solution)/shard_map/ppermute | solution.py:115
  258.3 33.6 %collective-permute-start.16 = (bf16[128,3072]{1,0:T(8,128)(2,1)}, bf16[128,3072]{1,0:T(8,128)(2,1)S(1)}, u32[]{:S(2)}, u32[]{:S(2)}) collective-permute-start(bf16[128,3072]{1,0:T(8,128)(2,1)} %collective-permute-done.15), channel_id=1, source_target_pairs={{0,1},{1,2},{2,3},{3,0},{4,5},{5,6},{6,7},{7,4},{8,9},{9,10},{10,1... | collective-permute-start | bytes 2359304 | tf_op jit(solution)/shard_map/ppermute | solution.py:115
  275.2 33.7 %collective-permute-start.13 = (bf16[128,3072]{1,0:T(8,128)(2,1)}, bf16[128,3072]{1,0:T(8,128)(2,1)}, u32[]{:S(2)}, u32[]{:S(2)}) collective-permute-start(bf16[128,3072]{1,0:T(8,128)(2,1)} %collective-permute-done.12), channel_id=1, source_target_pairs={{0,1},{1,2},{2,3},{3,0},{4,5},{5,6},{6,7},{7,4},{8,9},{9,10},{10,1... | collective-permute-start | bytes 2359304 | tf_op jit(solution)/shard_map/ppermute | solution.py:115
  291.9 33.7 %collective-permute-start.17 = (bf16[128,3072]{1,0:T(8,128)(2,1)S(1)}, bf16[128,3072]{1,0:T(8,128)(2,1)S(1)}, u32[]{:S(2)}, u32[]{:S(2)}) collective-permute-start(bf16[128,3072]{1,0:T(8,128)(2,1)S(1)} %collective-permute-done.16), channel_id=1, source_target_pairs={{0,1},{1,2},{2,3},{3,0},{4,5},{5,6},{6,7},{7,4},{8,9},{9,10},{10,1... | collective-permute-start | bytes 2359304 | tf_op jit(solution)/shard_map/ppermute | solution.py:115
  293.1 32.6 %copy-start = (bf16[4,128,3072]{2,1,0:T(8,128)(2,1)}, bf16[4,128,3072]{2,1,0:T(8,128)(2,1)S(1)}, u32[]{:S(2)}) copy-start(bf16[4,128,3072]{2,1,0:T(8,128)(2,1)S(1)} %bitcast_dynamic-update-slice_fusion.5) | copy-start | bytes 9437188
  308.9 34.0 %collective-permute-start.14 = (bf16[128,3072]{1,0:T(8,128)(2,1)}, bf16[128,3072]{1,0:T(8,128)(2,1)}, u32[]{:S(2)}, u32[]{:S(2)}) collective-permute-start(bf16[128,3072]{1,0:T(8,128)(2,1)} %collective-permute-done.13), channel_id=1, source_target_pairs={{0,1},{1,2},{2,3},{3,0},{4,5},{5,6},{6,7},{7,4},{8,9},{9,10},{10,1... | collective-permute-start | bytes 2359304 | tf_op jit(solution)/shard_map/ppermute | solution.py:115
  340.7 135.8 %reduce-scatter.6.cloned.1.call-start = ((), (), s32[]{:S(2)}) async-start(), calls=%async_computation.7 | async-start | bytes 3538944 | tf_op jit(solution)/shard_map/reduce_scatter | solution.py:146
  361.8 138.0 %reduce-scatter.4.cloned.1.call-start = ((), (), s32[]{:S(2)}) async-start(), calls=%async_computation.5 | async-start | bytes 7077888 | tf_op jit(solution)/shard_map/reduce_scatter | solution.py:146
  368.9 13.5 %collective-permute-start.6 = (bf16[256,1024]{1,0:T(8,128)(2,1)}, bf16[256,1024]{1,0:T(8,128)(2,1)S(1)}, u32[]{:S(2)}, u32[]{:S(2)}) collective-permute-start(bf16[256,1024]{1,0:T(8,128)(2,1)} %shard_map.84), channel_id=1, source_target_pairs={{0,1},{1,2},{2,3},{3,0},{4,5},{5,6},{6,7},{7,4},{8,9},{9,10},{10,1... | collective-permute-start | bytes 1572872 | tf_op jit(solution)/shard_map/ppermute | solution.py:115
  382.4 14.3 %collective-permute-start.7 = (bf16[256,1024]{1,0:T(8,128)(2,1)S(1)}, bf16[256,1024]{1,0:T(8,128)(2,1)S(1)}, u32[]{:S(2)}, u32[]{:S(2)}) collective-permute-start(bf16[256,1024]{1,0:T(8,128)(2,1)S(1)} %collective-permute-done.6), channel_id=1, source_target_pairs={{0,1},{1,2},{2,3},{3,0},{4,5},{5,6},{6,7},{7,4},{8,9},{9,10},{10,1... | collective-permute-start | bytes 1572872 | tf_op jit(solution)/shard_map/ppermute | solution.py:115
  396.7 11.0 %collective-permute-start.8 = (bf16[256,1024]{1,0:T(8,128)(2,1)S(1)}, bf16[256,1024]{1,0:T(8,128)(2,1)S(1)}, u32[]{:S(2)}, u32[]{:S(2)}) collective-permute-start(bf16[256,1024]{1,0:T(8,128)(2,1)S(1)} %collective-permute-done.7), channel_id=1, source_target_pairs={{0,1},{1,2},{2,3},{3,0},{4,5},{5,6},{6,7},{7,4},{8,9},{9,10},{10,1... | collective-permute-start | bytes 1572872 | tf_op jit(solution)/shard_map/ppermute | solution.py:115
  407.7 1.3 copy-start.2
  430.7 12.3 %copy-start.1 = (bf16[4,128,3072]{2,1,0:T(8,128)(2,1)S(1)}, bf16[4,128,3072]{2,1,0:T(8,128)(2,1)}, u32[]{:S(2)}) copy-start(bf16[4,128,3072]{2,1,0:T(8,128)(2,1)} %bitcast_dynamic-update-slice_fusion.3) | copy-start | bytes 9437188
Sparse Core Ops, SparseCore 0:
  10.5 35.0 all-gather.5
  48.0 32.3 all-gather.3
  82.2 45.5 all-gather.7
  340.9 43.4 reduce-scatter.7
  388.0 46.2 reduce-scatter.5
  438.0 61.7 reduce-scatter.3

commit v2 on v1

--- a/solution.py
+++ b/solution.py
@@ -76,11 +76,13 @@
     )(positions.reshape(seq_len, 1), *arrays)
 
 
-def qkv_weight_kernel(heads, head, tokens_ref, grads_ref, out_ref):
-    block = tokens_ref.shape[1]
-    left = tokens_ref[...].T
+def qkv_weight_kernel(heads, head, *refs):
+    token_refs, grad_refs, out_ref = refs[:PIECES], refs[PIECES:-1], refs[-1]
+    block = out_ref.shape[0] // (3 * heads)
+    lefts = [ref[...].T for ref in token_refs]
     for pair in range(heads * 3 // 2):
-        term = dot_f32(left, grads_ref[:, 2 * pair * head : (2 * pair + 2) * head])
+        at = slice(2 * pair * head, (2 * pair + 2) * head)
+        term = sum(dot_f32(left, ref[:, at]) for left, ref in zip(lefts, grad_refs))
         for half in range(2):
             at_head, part = divmod(2 * pair + half, 3)
             out_ref[pl.ds(part * heads + at_head, block, stride=3 * heads), :] = term[
@@ -88,26 +90,24 @@
             ]
 
 
-def qkv_weight_grad(tokens_all, grads_all, heads, head):
-    count, width = tokens_all.shape
-    columns = grads_all.shape[1]
+def qkv_weight_grad(tokens_parts, grads_parts, heads, head):
+    count, width = tokens_parts[0].shape
+    columns = grads_parts[0].shape[1]
     block = 256
     rows = pl.pallas_call(
         functools.partial(qkv_weight_kernel, heads, head),
         grid=(width // block,),
-        in_specs=[
-            pl.BlockSpec((count, block), lambda i: (0, i)),
-            pl.BlockSpec((count, columns), lambda i: (0, 0)),
-        ],
+        in_specs=[pl.BlockSpec((count, block), lambda i: (0, i))] * PIECES
+        + [pl.BlockSpec((count, columns), lambda i: (0, 0))] * PIECES,
         out_specs=pl.BlockSpec((block * 3 * heads, head), lambda i: (i, 0)),
         out_shape=jax.ShapeDtypeStruct((width * 3 * heads, head), jnp.float32),
         cost_estimate=pl.CostEstimate(
-            flops=2 * count * width * columns,
-            bytes_accessed=4 * width * columns + 2 * count * (width + columns),
+            flops=2 * PIECES * count * width * columns,
+            bytes_accessed=4 * width * columns + 2 * PIECES * count * (width + columns),
             transcendentals=0,
         ),
         compiler_params=pltpu.CompilerParams(vmem_limit_bytes=VMEM_LIMIT),
-    )(tokens_all, grads_all)
+    )(*tokens_parts, *grads_parts)
     return rows.reshape(width, 3, heads, head).transpose(0, 2, 1, 3)
 
 
@@ -132,10 +132,18 @@
     me = lax.axis_index("depth")
     out = jnp.zeros((size,) + block.shape, block.dtype)
     out = lax.dynamic_update_index_in_dim(out, block, me, 0)
+    arrivals = []
     for step in range(1, size):
         block = send_on(block, size)
+        arrivals.append(block)
         out = lax.dynamic_update_index_in_dim(out, block, lax.rem(me + size - step, size), 0)
-    return out
+    return out, arrivals
+
+
+def after(block, *earlier):
+    for other in earlier:
+        block = block + (other[:1, :1] * jnp.zeros((), other.dtype)).astype(block.dtype)
+    return block
 
 
 def gather_rows(local_rows):
@@ -146,7 +154,41 @@
     return lax.psum_scatter(whole, ("row", "col"), scatter_dimension=0, tiled=True)
 
 
-def per_device(size, tokens, w_qkv, w_out, positions, d_output):
+def swap(block, mask, group):
+    return lax.ppermute(block, ("row", "col"), [(i, i ^ mask) for i in range(group)])
+
+
+def gather_direct(block, group, core):
+    me = lax.axis_index(("row", "col"))
+    masks = [m for m in range(group) if not m & core]
+    out = jnp.zeros((group,) + block.shape, block.dtype)
+    from_chips = [swap(block, m, group) if m else block for m in masks]
+    for mask, arrived in zip(masks, from_chips):
+        out = lax.dynamic_update_index_in_dim(out, arrived, me ^ mask, 0)
+        other = swap(arrived, core, group)
+        out = lax.dynamic_update_index_in_dim(out, other, me ^ (mask | core), 0)
+    return out.reshape(group * block.shape[0], block.shape[1]), from_chips[-1]
+
+
+def scatter_direct(whole, group, core):
+    me = lax.axis_index(("row", "col"))
+    masks = [m for m in range(group) if not m & core]
+    blocks = whole.reshape(group, whole.shape[0] // group, whole.shape[1])
+
+    def block(mask):
+        return lax.dynamic_index_in_dim(blocks, me ^ mask, 0, False)
+
+    total = 0.0
+    for mask in reversed(masks):
+        arrived = swap(block(mask | core), core, group)
+        chip_sum = block(mask).astype(jnp.float32) + arrived.astype(jnp.float32)
+        if mask:
+            chip_sum = swap(chip_sum.astype(jnp.bfloat16), mask, group).astype(jnp.float32)
+        total = total + chip_sum
+    return total.astype(jnp.bfloat16)
+
+
+def per_device(size, group, core, tokens, w_qkv, w_out, positions, d_output):
     seq_len = positions.shape[0]
     width, heads, _, head = w_qkv.shape
     hidden = heads * head
@@ -157,9 +199,13 @@
     qkv_flat = w_qkv.reshape(width, columns)
     out_flat = w_out.reshape(hidden, width)
 
-    gathered = [
-        gather_rows(tokens[p * part_rows : (p + 1) * part_rows]) for p in range(PIECES)
-    ]
+    gathered = []
+    last_arrival = None
+    for p in range(PIECES):
+        part = tokens[p * part_rows : (p + 1) * part_rows]
+        part = part if last_arrival is None else after(part, last_arrival)
+        whole, last_arrival = gather_direct(part, group, core)
+        gathered.append(whole)
     pieces = []
     for piece in gathered:
         partial = dot_f32(piece, qkv_flat)
@@ -167,32 +213,35 @@
     projected = jnp.stack([p.reshape(sharers, part_rows, columns) for p in pieces], axis=1)
     projected = projected.reshape(seq_len, columns)
 
-    grad_all = gather_rows(d_output)
+    grad_all = gather_rows(after(d_output, last_arrival))
     d_mixed = dot_f32(grad_all, out_flat, CONTRACT_LAST)
     d_mixed = ring_sum(d_mixed.reshape(size, seq_len, hidden), size)
 
     mixed = attention_call(attend_kernel, positions, head, heads, False, projected)
-    heads_all = ring_gather(mixed, size).reshape(size * seq_len, hidden)
-    output = scatter_rows(dot_f32(heads_all, out_flat).astype(jnp.bfloat16))
+    heads_all, mixed_arrivals = ring_gather(mixed, size)
+    heads_all = heads_all.reshape(size * seq_len, hidden)
+    output_terms = dot_f32(heads_all, out_flat).astype(jnp.bfloat16)
+    output = scatter_rows(output_terms)
 
     grads = attention_call(
-        attend_back_kernel, positions, head, heads, True, projected, d_mixed
+        attend_back_kernel, positions, head, heads, True, projected, after(d_mixed, mixed_arrivals[-1])
     )
     d_out_weight = dot_f32(heads_all, grad_all, CONTRACT_FIRST)
 
     grads = grads.reshape(sharers, PIECES, part_rows, columns)
     all_grads = []
     d_tokens = []
+    arrivals = None
     for p in range(PIECES):
-        piece = ring_gather(grads[:, p].reshape(sharers * part_rows, columns), size)
+        own = grads[:, p].reshape(sharers * part_rows, columns)
+        own = own if arrivals is None else after(own, arrivals[-2], output_terms)
+        piece, arrivals = ring_gather(own, size)
         piece = piece.reshape(size * sharers * part_rows, columns)
         all_grads.append(piece)
-        d_tokens.append(
-            scatter_rows(dot_f32(piece, qkv_flat, CONTRACT_LAST).astype(jnp.bfloat16))
-        )
-    d_qkv_weight = qkv_weight_grad(
-        jnp.concatenate(gathered, axis=0), jnp.concatenate(all_grads, axis=0), heads, head
-    )
+        terms = dot_f32(piece, qkv_flat, CONTRACT_LAST).astype(jnp.bfloat16)
+        terms = after(terms, d_out_weight)
+        d_tokens.append(scatter_direct(terms, group, core))
+    d_qkv_weight = qkv_weight_grad(gathered, all_grads, heads, head)
     return (
         output,
         jnp.concatenate(d_tokens, axis=0),
@@ -203,7 +252,12 @@
 
 def solution(mesh):
     return jax.shard_map(
-        functools.partial(per_device, mesh.shape["depth"]),
+        functools.partial(
+            per_device,
+            mesh.shape["depth"],
+            mesh.shape["row"] * mesh.shape["col"],
+            mesh.shape["col"],
+        ),
         mesh=mesh,
         in_specs=(
             P(("row", "col"), "depth"),

time: 508 us -> 485 us (0.955)
  waiting for transfers between devices: 269 us -> 218 us
  starting transfers between devices: 6.44 us -> 23.7 us
  local copies, waits for them, and re-layouts: 52.1 us -> 67 us
  matrix products: 94.8 us -> 85.6 us
    all_gather x3 -> x1, waiting for transfers between devices: 26.6 us -> 0.01 us  [gather_rows(): return lax.all_gather(local_rows, ('row', 'col'), axis=0, tiled=True)]
    reduce_scatter x3 -> x1, waiting for transfers between devices: 21.2 us -> 0.01 us  [scatter_rows(): lax.psum_scatter(whole, ('row', 'col'), scatter_dimension=0, tiled=True)]
    ppermute x0 -> x28, starting transfers between devices: none -> 18.4 us  [swap(): lax.ppermute(block, ('row', 'col'), [(i, i ^ mask) for i in range(group)])]
    ppermute x18, waiting for transfers between devices: 220 us -> 202 us  [send_on(): lax.ppermute(block, 'depth', [(i, (i + 1) % size) for i in range(size)])]
    ppermute x0 -> x28, waiting for transfers between devices: none -> 16 us  [swap(): lax.ppermute(block, ('row', 'col'), [(i, i ^ mask) for i in range(group)])]
    dynamic_update_slice x0 -> x15, local copies, waits for them, and re-layouts: none -> 14.8 us  [the longest x7 8.56 us: gather_direct(): out = lax.dynamic_update_index_in_dim(out, arrived, me ^ mask, 0)]
    dot_general x7, matrix products: 94.8 us -> 85.6 us  [dot_f32(): lax.dot_general(left, right, dims, preferred_element_type=jnp.float32)]
    concatenate x2 -> x0, other arithmetic: 9.03 us -> none  [the longest x1 5.95 us: per_device(): jnp.concatenate(gathered, axis=0)]
  transfers between devices with their start and end apart: 24 -> 48, of which waited for: 17 -> 17; matrix products, arithmetic and copies ran while one was open for 31% -> 35% of each run, Pallas kernels for 7% -> 9%
where the time goes in v2:
time: 485 us; the launch traced here: 482 us
  waiting for transfers between devices  218 us (45%)
  matrix products  85.6 us (18%)
  local copies, waits for them, and re-layouts  67 us (14%)
  Pallas kernels  45.3 us (9%)
  other arithmetic  24.4 us (5%)
  starting transfers between devices  23.7 us (5%)
  between operations  18.6 us (4%)
    ppermute x18, waiting for transfers between devices, send_on(): lax.ppermute(block, 'depth', [(i, (i + 1) % size) for i in range(size)])  202 us
    dot_general x7, matrix products, dot_f32(): lax.dot_general(left, right, dims, preferred_element_type=jnp.float32)  85.6 us
    unnamed x39, local copies, waits for them, and re-layouts  31.3 us
    pallas_call x1, Pallas kernels, qkv_weight_grad(): pl.pallas_call(functools.partial(qkv_weight_kernel, heads, head), grid=(w...  29.7 us
    ppermute x28, starting transfers between devices, swap(): lax.ppermute(block, ('row', 'col'), [(i, i ^ mask) for i in range(group)])  18.4 us
    ppermute x28, waiting for transfers between devices, swap(): lax.ppermute(block, ('row', 'col'), [(i, i ^ mask) for i in range(group)])  16 us
    pallas_call x2, Pallas kernels, attention_call(): pl.pallas_call(functools.partial(kernel, score_scale, head), grid=(heads,...  15.6 us
    convert_element_type x8, other arithmetic, ring_sum(): running = (arrived + chunk(1 + step)).astype(jnp.bfloat16)  12.5 us
  transfers between devices with their start and end apart: 48, of which 17 were waited for; matrix products, arithmetic and copies ran while one was open for 35% of the time, Pallas kernels for 9%

profile of v2, /device:TPU:0, one launch (start us, length us, event | category | flops | bytes accessed | tf_op | source)
XLA Modules:
  0.0 482.5 jit_solution(15412166391043024744)
XLA Ops:
  8.2 3.0 collective-permute-start.3
  12.8 24.1 %copy.11 = bf16[3072,8,3,128]{0,3,2,1:T(8,128)(2,1)} copy(bf16[3072,8,3,128]{3,1,2,0:T(8,128)(2,1)} %param.6) | data formatting | bytes 37748736 | tf_op args[1]
  48.9 15.8 %collective-permute-done.15 = bf16[64,3072]{1,0:T(8,128)(2,1)S(1)} collective-permute-done((bf16[64,3072]{1,0:T(8,128)(2,1)}, bf16[64,3072]{1,0:T(8,128)(2,1)S(1)}, u32[]{:S(2)}, u32[]{:S(2)}) %collective-permute-start.15) | collective-permute-done | bytes 393248 | tf_op jit(solution)/shard_map/ppermute | solution.py:158
  73.0 14.9 %fusion.26 = f32[4,128,3072]{2,1,0:T(8,128)S(1)} fusion(bf16[4,128,3072]{2,1,0:T(8,128)(2,1)} %bitcast.206, bf16[3072,3072,1]{0,1,2:T(8,128)(2,1)} %bitcast.190), kind=kOutput, calls=%fused_computation.90 | convolution fusion | flops 9663676416 | bytes 28311552 | tf_op jit(solution)/shard_map/dot_general | solution.py:18
  98.7 14.2 %fusion.27 = f32[4,128,3072]{2,1,0:T(8,128)S(1)} fusion(bf16[4,128,3072]{2,1,0:T(8,128)(2,1)} %bitcast.27, bf16[3072,3072,1]{0,1,2:T(8,128)(2,1)} %bitcast.191), kind=kOutput, calls=%fused_computation.91 | convolution fusion | flops 9663676416 | bytes 28311552 | tf_op jit(solution)/shard_map/dot_general | solution.py:18
  112.9 2.7 copy-done.2
  120.7 17.2 %collective-permute-done.17 = bf16[128,3072]{1,0:T(8,128)(2,1)S(1)} collective-permute-done((bf16[128,3072]{1,0:T(8,128)(2,1)S(1)}, bf16[128,3072]{1,0:T(8,128)(2,1)S(1)}, u32[]{:S(2)}, u32[]{:S(2)}) %collective-permute-start.17) | collective-permute-done | bytes 786464 | tf_op jit(solution)/shard_map/ppermute | solution.py:115
  139.5 15.3 %collective-permute-done.8 = bf16[128,3072]{1,0:T(8,128)(2,1)} collective-permute-done((bf16[128,3072]{1,0:T(8,128)(2,1)S(1)}, bf16[128,3072]{1,0:T(8,128)(2,1)}, u32[]{:S(2)}, u32[]{:S(2)}) %collective-permute-start.8) | collective-permute-done | bytes 786464 | tf_op jit(solution)/shard_map/ppermute | solution.py:115
  156.7 14.9 %collective-permute-done.18 = bf16[128,3072]{1,0:T(8,128)(2,1)S(1)} collective-permute-done((bf16[128,3072]{1,0:T(8,128)(2,1)S(1)}, bf16[128,3072]{1,0:T(8,128)(2,1)S(1)}, u32[]{:S(2)}, u32[]{:S(2)}) %collective-permute-start.18) | collective-permute-done | bytes 786464 | tf_op jit(solution)/shard_map/ppermute | solution.py:115
  174.0 14.4 %collective-permute-done.9 = bf16[128,3072]{1,0:T(8,128)(2,1)S(1)} collective-permute-done((bf16[128,3072]{1,0:T(8,128)(2,1)S(1)}, bf16[128,3072]{1,0:T(8,128)(2,1)S(1)}, u32[]{:S(2)}, u32[]{:S(2)}) %collective-permute-start.9) | collective-permute-done | bytes 786464 | tf_op jit(solution)/shard_map/ppermute | solution.py:115
  190.0 14.8 %collective-permute-done.19 = bf16[128,3072]{1,0:T(8,128)(2,1)S(1)} collective-permute-done((bf16[128,3072]{1,0:T(8,128)(2,1)S(1)}, bf16[128,3072]{1,0:T(8,128)(2,1)S(1)}, u32[]{:S(2)}, u32[]{:S(2)}) %collective-permute-start.19) | collective-permute-done | bytes 786464 | tf_op jit(solution)/shard_map/ppermute | solution.py:115
  207.7 7.0 %shard_map.84 = bf16[256,1024]{1,0:T(8,128)(2,1)} custom-call(s32[256,1]{1,0:T(8,128)} %copy.16.positions_ref, bf16[256,3072]{1,0:T(8,128)(2,1)} %bitcast.196), custom_call_target="tpu_custom_call" | custom-call | flops 268435456 | bytes 2097152 | tf_op jit(solution)/shard_map/pallas_call | solution.py:63
  214.7 15.6 %collective-permute-done.20 = bf16[256,1024]{1,0:T(8,128)(2,1)} collective-permute-done((bf16[256,1024]{1,0:T(8,128)(2,1)}, bf16[256,1024]{1,0:T(8,128)(2,1)}, u32[]{:S(2)}, u32[]{:S(2)}) %collective-permute-start.20) | collective-permute-done | bytes 524320 | tf_op jit(solution)/shard_map/ppermute | solution.py:115
  230.3 10.7 %fusion.28 = f32[4,256,1024]{2,1,0:T(8,128)S(1)} fusion(bf16[4,256,3072]{2,1,0:T(8,128)(2,1)} %bitcast.221, bf16[1024,3072,1]{1,0,2:T(8,128)(2,1)} %bitcast.219), kind=kOutput, calls=%fused_computation.92 | convolution fusion | flops 6442450944 | bytes 16777216 | tf_op jit(solution)/shard_map/dot_general | solution.py:18
  245.0 15.7 %collective-permute-done.23 = bf16[256,1024]{1,0:T(8,128)(2,1)S(1)} collective-permute-done((bf16[256,1024]{1,0:T(8,128)(2,1)}, bf16[256,1024]{1,0:T(8,128)(2,1)S(1)}, u32[]{:S(2)}, u32[]{:S(2)}) %collective-permute-start.23) | collective-permute-done | bytes 524320 | tf_op jit(solution)/shard_map/ppermute | solution.py:115
  264.4 7.6 %collective-permute-done.22 = bf16[256,1024]{1,0:T(8,128)(2,1)S(1)} collective-permute-done((bf16[256,1024]{1,0:T(8,128)(2,1)}, bf16[256,1024]{1,0:T(8,128)(2,1)S(1)}, u32[]{:S(2)}, u32[]{:S(2)}) %collective-permute-start.22) | collective-permute-done | bytes 524320 | tf_op jit(solution)/shard_map/ppermute | solution.py:115
  272.0 8.9 %collective-permute-done.24 = bf16[256,1024]{1,0:T(8,128)(2,1)S(1)} collective-permute-done((bf16[256,1024]{1,0:T(8,128)(2,1)S(1)}, bf16[256,1024]{1,0:T(8,128)(2,1)S(1)}, u32[]{:S(2)}, u32[]{:S(2)}) %collective-permute-start.24) | collective-permute-done | bytes 524320 | tf_op jit(solution)/shard_map/ppermute | solution.py:115
  282.4 11.4 %convolution_convert_fusion = bf16[1024,3072]{1,0:T(8,128)(2,1)} fusion(bf16[1024,1024]{1,0:T(8,128)(2,1)S(1)} %bitcast.216, bf16[1024,3072]{1,0:T(8,128)(2,1)} %bitcast.220), kind=kOutput, calls=%fused_computation | convolution fusion | flops 6445596672 | bytes 14680064 | tf_op jit(solution)/shard_map/dot_general | solution.py:18
  299.7 8.6 %shard_map.85 = bf16[256,3072]{1,0:T(8,128)(2,1)} custom-call(s32[256,1]{1,0:T(8,128)} %copy.16.positions_ref, bf16[256,3072]{1,0:T(8,128)(2,1)} %bitcast.197, bf16[256,1024]{1,0:T(8,128)(2,1)} %fusion.25.d_mixed_ref), custom_call_target="tpu_custom_call" | custom-call | flops 939524096 | bytes 6291456 | tf_op jit(solution)/shard_map/pallas_call | solution.py:63
  309.8 12.8 %fusion.29 = f32[1024,3072]{1,0:T(8,128)} fusion(bf16[1024,1024]{1,0:T(8,128)(2,1)S(1)} %bitcast.217, bf16[1024,3072]{1,0:T(8,128)(2,1)} %all-gather.2.cloned.1.call-done), kind=kOutput, calls=%fused_computation.93 | convolution fusion | flops 6442450944 | bytes 20971520 | tf_op jit(solution)/shard_map/dot_general | solution.py:18
  324.5 4.0 collective-permute-done.26
  329.1 17.4 %collective-permute-done.27 = bf16[128,3072]{1,0:T(8,128)(2,1)S(1)} collective-permute-done((bf16[128,3072]{1,0:T(8,128)(2,1)S(1)}, bf16[128,3072]{1,0:T(8,128)(2,1)S(1)}, u32[]{:S(2)}, u32[]{:S(2)}) %collective-permute-start.27) | collective-permute-done | bytes 786464 | tf_op jit(solution)/shard_map/ppermute | solution.py:115
  350.3 32.4 %collective-permute-done.28 = bf16[128,3072]{1,0:T(8,128)(2,1)S(1)} collective-permute-done((bf16[128,3072]{1,0:T(8,128)(2,1)S(1)}, bf16[128,3072]{1,0:T(8,128)(2,1)S(1)}, u32[]{:S(2)}, u32[]{:S(2)}) %collective-permute-start.28) | collective-permute-done | bytes 786464 | tf_op jit(solution)/shard_map/ppermute | solution.py:115
  382.8 11.4 %fusion = bf16[512,3072]{1,0:T(8,128)(2,1)} fusion(bf16[512,3072]{1,0:T(8,128)(2,1)S(1)} %bitcast.204, bf16[3072,3072]{0,1:T(8,128)(2,1)S(1)} %bitcast.194, bf16[]{:T(256)} %bitcast.57), kind=kOutput, calls=%fused_computation.3 | convolution fusion | flops 9666822144 | bytes 25165826 | tf_op jit(solution)/shard_map/dot_general | solution.py:18
  394.2 2.3 dynamic-slice_bitcast_fusion.7
  398.7 13.4 %collective-permute-done.37 = bf16[128,3072]{1,0:T(8,128)(2,1)S(1)} collective-permute-done((bf16[128,3072]{1,0:T(8,128)(2,1)}, bf16[128,3072]{1,0:T(8,128)(2,1)S(1)}, u32[]{:S(2)}, u32[]{:S(2)}) %collective-permute-start.37) | collective-permute-done | bytes 786464 | tf_op jit(solution)/shard_map/ppermute | solution.py:115
  412.1 2.4 fusion.23
  414.7 3.0 collective-permute-start.34
  418.1 9.3 %collective-permute-done.38 = bf16[128,3072]{1,0:T(8,128)(2,1)S(1)} collective-permute-done((bf16[128,3072]{1,0:T(8,128)(2,1)S(1)}, bf16[128,3072]{1,0:T(8,128)(2,1)S(1)}, u32[]{:S(2)}, u32[]{:S(2)}) %collective-permute-start.38) | collective-permute-done | bytes 786464 | tf_op jit(solution)/shard_map/ppermute | solution.py:115
  427.4 10.2 %fusion.1 = bf16[512,3072]{1,0:T(8,128)(2,1)S(1)} fusion(bf16[512,3072]{1,0:T(8,128)(2,1)S(1)} %bitcast.202, bf16[3072,3072]{0,1:T(8,128)(2,1)S(1)} %bitcast.195, bf16[]{:T(256)} %bitcast.57), kind=kOutput, calls=%fused_computation.4 | convolution fusion | flops 9666822144 | bytes 25165826 | tf_op jit(solution)/shard_map/dot_general | solution.py:18
  441.2 3.3 collective-permute-start.44
  444.7 29.7 %shard_map.86 = f32[73728,128]{1,0:T(8,128)} custom-call(bf16[512,3072]{1,0:T(8,128)(2,1)} %bitcast.207, bf16[512,3072]{1,0:T(8,128)(2,1)} %bitcast.85.refs_1_, bf16[512,3072]{1,0:T(8,128)(2,1)} %bitcast.205, bf16[512,3072]{1,0:T(8,128)(2,1)} %bitcast.203), custom_call_target="tpu_custom_call" | custom-call | flops 19327352832 | bytes 50331648 | tf_op jit(solution)/shard_map/pallas_call | solution.py:97
  (180 shorter events, 75.4 us)
Async XLA Ops:
  7.2 223.2 %all-gather.2.cloned.1.call-start = ((), (), s32[]{:S(2)}) async-start(), calls=%async_computation.2 | async-start | bytes 7077888 | tf_op jit(solution)/shard_map/all_gather | solution.py:150
  8.2 59.4 %collective-permute-start.3 = (bf16[64,3072]{1,0:T(8,128)(2,1)S(1)}, bf16[64,3072]{1,0:T(8,128)(2,1)}, u32[]{:S(2)}, u32[]{:S(2)}) collective-permute-start(bf16[64,3072]{1,0:T(8,128)(2,1)S(1)} %slice.31), channel_id=1, source_target_pairs={{0,16},{4,20},{8,24},{12,28},{16,0},{20,4},{24,8},{28,12},{1,17},{... | collective-permute-start | bytes 1179656 | tf_op jit(solution)/shard_map/ppermute | solution.py:158
  11.2 36.5 %collective-permute-start.1 = (bf16[64,3072]{1,0:T(8,128)(2,1)S(1)}, bf16[64,3072]{1,0:T(8,128)(2,1)}, u32[]{:S(2)}, u32[]{:S(2)}) collective-permute-start(bf16[64,3072]{1,0:T(8,128)(2,1)S(1)} %slice.31), channel_id=1, source_target_pairs={{0,4},{4,0},{8,12},{12,8},{16,20},{20,16},{24,28},{28,24},{1,5},{5... | collective-permute-start | bytes 1179656 | tf_op jit(solution)/shard_map/ppermute | solution.py:158
  12.8 34.0 %collective-permute-start = (bf16[64,3072]{1,0:T(8,128)(2,1)S(1)}, bf16[64,3072]{1,0:T(8,128)(2,1)}, u32[]{:S(2)}, u32[]{:S(2)}) collective-permute-start(bf16[64,3072]{1,0:T(8,128)(2,1)S(1)} %slice.31), channel_id=1, source_target_pairs={{0,8},{4,12},{8,0},{12,4},{16,24},{20,28},{24,16},{28,20},{1,9},{5... | collective-permute-start | bytes 1179656 | tf_op jit(solution)/shard_map/ppermute | solution.py:158
  12.8 25.6 %collective-permute-start.5 = (bf16[64,3072]{1,0:T(8,128)(2,1)S(1)}, bf16[64,3072]{1,0:T(8,128)(2,1)}, u32[]{:S(2)}, u32[]{:S(2)}) collective-permute-start(bf16[64,3072]{1,0:T(8,128)(2,1)S(1)} %slice.31), channel_id=1, source_target_pairs={{0,20},{4,16},{8,28},{12,24},{16,4},{20,0},{24,12},{28,8},{1,21},{... | collective-permute-start | bytes 1179656 | tf_op jit(solution)/shard_map/ppermute | solution.py:158
  43.2 46.3 %collective-permute-start.13 = (bf16[64,3072]{1,0:T(8,128)(2,1)}, bf16[64,3072]{1,0:T(8,128)(2,1)}, u32[]{:S(2)}, u32[]{:S(2)}) collective-permute-start(bf16[64,3072]{1,0:T(8,128)(2,1)} %get-tuple-element.5), channel_id=1, source_target_pairs={{0,16},{4,20},{8,24},{12,28},{16,0},{20,4},{24,8},{28,12},{1,17},{... | collective-permute-start | bytes 1179656 | tf_op jit(solution)/shard_map/ppermute | solution.py:158
  45.2 44.8 %collective-permute-start.11 = (bf16[64,3072]{1,0:T(8,128)(2,1)}, bf16[64,3072]{1,0:T(8,128)(2,1)}, u32[]{:S(2)}, u32[]{:S(2)}) collective-permute-start(bf16[64,3072]{1,0:T(8,128)(2,1)} %get-tuple-element.5), channel_id=1, source_target_pairs={{0,4},{4,0},{8,12},{12,8},{16,20},{20,16},{24,28},{28,24},{1,5},{5... | collective-permute-start | bytes 1179656 | tf_op jit(solution)/shard_map/ppermute | solution.py:158
  46.7 43.4 %collective-permute-start.10 = (bf16[64,3072]{1,0:T(8,128)(2,1)}, bf16[64,3072]{1,0:T(8,128)(2,1)}, u32[]{:S(2)}, u32[]{:S(2)}) collective-permute-start(bf16[64,3072]{1,0:T(8,128)(2,1)} %get-tuple-element.5), channel_id=1, source_target_pairs={{0,8},{4,12},{8,0},{12,4},{16,24},{20,28},{24,16},{28,20},{1,9},{5... | collective-permute-start | bytes 1179656 | tf_op jit(solution)/shard_map/ppermute | solution.py:158
  47.8 16.9 %collective-permute-start.15 = (bf16[64,3072]{1,0:T(8,128)(2,1)}, bf16[64,3072]{1,0:T(8,128)(2,1)S(1)}, u32[]{:S(2)}, u32[]{:S(2)}) collective-permute-start(bf16[64,3072]{1,0:T(8,128)(2,1)} %get-tuple-element.5), channel_id=1, source_target_pairs={{0,20},{4,16},{8,28},{12,24},{16,4},{20,0},{24,12},{28,8},{1,21},{... | collective-permute-start | bytes 1179656 | tf_op jit(solution)/shard_map/ppermute | solution.py:158
  67.6 408.1 %reduce-scatter.2.cloned.1.call-start = ((), (), s32[]{:S(2)}) async-start(), calls=%async_computation.1 | async-start | bytes 7077888 | tf_op jit(solution)/shard_map/reduce_scatter | solution.py:154
  88.0 29.2 %collective-permute-start.7 = (bf16[128,3072]{1,0:T(8,128)(2,1)S(1)}, bf16[128,3072]{1,0:T(8,128)(2,1)}, u32[]{:S(2)}, u32[]{:S(2)}) collective-permute-start(bf16[128,3072]{1,0:T(8,128)(2,1)S(1)} %fusion.11), channel_id=1, source_target_pairs={{0,1},{1,2},{2,3},{3,0},{4,5},{5,6},{6,7},{7,4},{8,9},{9,10},{10,1... | collective-permute-start | bytes 2359304 | tf_op jit(solution)/shard_map/ppermute | solution.py:115
  115.7 22.2 %collective-permute-start.17 = (bf16[128,3072]{1,0:T(8,128)(2,1)S(1)}, bf16[128,3072]{1,0:T(8,128)(2,1)S(1)}, u32[]{:S(2)}, u32[]{:S(2)}) collective-permute-start(bf16[128,3072]{1,0:T(8,128)(2,1)S(1)} %fusion.12), channel_id=1, source_target_pairs={{0,1},{1,2},{2,3},{3,0},{4,5},{5,6},{6,7},{7,4},{8,9},{9,10},{10,1... | collective-permute-start | bytes 2359304 | tf_op jit(solution)/shard_map/ppermute | solution.py:115
  119.0 35.8 %collective-permute-start.8 = (bf16[128,3072]{1,0:T(8,128)(2,1)S(1)}, bf16[128,3072]{1,0:T(8,128)(2,1)}, u32[]{:S(2)}, u32[]{:S(2)}) collective-permute-start(bf16[128,3072]{1,0:T(8,128)(2,1)S(1)} %fusion.7), channel_id=1, source_target_pairs={{0,1},{1,2},{2,3},{3,0},{4,5},{5,6},{6,7},{7,4},{8,9},{9,10},{10,1... | collective-permute-start | bytes 2359304 | tf_op jit(solution)/shard_map/ppermute | solution.py:115
  139.4 32.1 %collective-permute-start.18 = (bf16[128,3072]{1,0:T(8,128)(2,1)S(1)}, bf16[128,3072]{1,0:T(8,128)(2,1)S(1)}, u32[]{:S(2)}, u32[]{:S(2)}) collective-permute-start(bf16[128,3072]{1,0:T(8,128)(2,1)S(1)} %fusion.4), channel_id=1, source_target_pairs={{0,1},{1,2},{2,3},{3,0},{4,5},{5,6},{6,7},{7,4},{8,9},{9,10},{10,1... | collective-permute-start | bytes 2359304 | tf_op jit(solution)/shard_map/ppermute | solution.py:115
  156.6 31.8 %collective-permute-start.9 = (bf16[128,3072]{1,0:T(8,128)(2,1)S(1)}, bf16[128,3072]{1,0:T(8,128)(2,1)S(1)}, u32[]{:S(2)}, u32[]{:S(2)}) collective-permute-start(bf16[128,3072]{1,0:T(8,128)(2,1)S(1)} %fusion.6), channel_id=1, source_target_pairs={{0,1},{1,2},{2,3},{3,0},{4,5},{5,6},{6,7},{7,4},{8,9},{9,10},{10,1... | collective-permute-start | bytes 2359304 | tf_op jit(solution)/shard_map/ppermute | solution.py:115
  173.1 31.7 %collective-permute-start.19 = (bf16[128,3072]{1,0:T(8,128)(2,1)S(1)}, bf16[128,3072]{1,0:T(8,128)(2,1)S(1)}, u32[]{:S(2)}, u32[]{:S(2)}) collective-permute-start(bf16[128,3072]{1,0:T(8,128)(2,1)S(1)} %fusion.3), channel_id=1, source_target_pairs={{0,1},{1,2},{2,3},{3,0},{4,5},{5,6},{6,7},{7,4},{8,9},{9,10},{10,1... | collective-permute-start | bytes 2359304 | tf_op jit(solution)/shard_map/ppermute | solution.py:115
  243.9 16.9 %collective-permute-start.23 = (bf16[256,1024]{1,0:T(8,128)(2,1)}, bf16[256,1024]{1,0:T(8,128)(2,1)S(1)}, u32[]{:S(2)}, u32[]{:S(2)}) collective-permute-start(bf16[256,1024]{1,0:T(8,128)(2,1)} %fusion.24), channel_id=1, source_target_pairs={{0,1},{1,2},{2,3},{3,0},{4,5},{5,6},{6,7},{7,4},{8,9},{9,10},{10,1... | collective-permute-start | bytes 1572872 | tf_op jit(solution)/shard_map/ppermute | solution.py:115
  245.0 27.0 %collective-permute-start.22 = (bf16[256,1024]{1,0:T(8,128)(2,1)}, bf16[256,1024]{1,0:T(8,128)(2,1)S(1)}, u32[]{:S(2)}, u32[]{:S(2)}) collective-permute-start(bf16[256,1024]{1,0:T(8,128)(2,1)} %collective-permute-done.21), channel_id=1, source_target_pairs={{0,1},{1,2},{2,3},{3,0},{4,5},{5,6},{6,7},{7,4},{8,9},{9,10},{10,1... | collective-permute-start | bytes 1572872 | tf_op jit(solution)/shard_map/ppermute | solution.py:115
  262.1 18.8 %collective-permute-start.24 = (bf16[256,1024]{1,0:T(8,128)(2,1)S(1)}, bf16[256,1024]{1,0:T(8,128)(2,1)S(1)}, u32[]{:S(2)}, u32[]{:S(2)}) collective-permute-start(bf16[256,1024]{1,0:T(8,128)(2,1)S(1)} %fusion.10), channel_id=1, source_target_pairs={{0,1},{1,2},{2,3},{3,0},{4,5},{5,6},{6,7},{7,4},{8,9},{9,10},{10,1... | collective-permute-start | bytes 1572872 | tf_op jit(solution)/shard_map/ppermute | solution.py:115
  309.6 18.9 %collective-permute-start.26 = (bf16[128,3072]{1,0:T(8,128)(2,1)S(1)}, bf16[128,3072]{1,0:T(8,128)(2,1)S(1)}, u32[]{:S(2)}, u32[]{:S(2)}) collective-permute-start(bf16[128,3072]{1,0:T(8,128)(2,1)S(1)} %bitcast.200), channel_id=1, source_target_pairs={{0,1},{1,2},{2,3},{3,0},{4,5},{5,6},{6,7},{7,4},{8,9},{9,10},{10,1... | collective-permute-start | bytes 2359304 | tf_op jit(solution)/shard_map/ppermute | solution.py:115
  328.5 17.9 %collective-permute-start.27 = (bf16[128,3072]{1,0:T(8,128)(2,1)S(1)}, bf16[128,3072]{1,0:T(8,128)(2,1)S(1)}, u32[]{:S(2)}, u32[]{:S(2)}) collective-permute-start(bf16[128,3072]{1,0:T(8,128)(2,1)S(1)} %collective-permute-done.26), channel_id=1, source_target_pairs={{0,1},{1,2},{2,3},{3,0},{4,5},{5,6},{6,7},{7,4},{8,9},{9,10},{10,1... | collective-permute-start | bytes 2359304 | tf_op jit(solution)/shard_map/ppermute | solution.py:115
  348.6 45.6 %collective-permute-start.36 = (bf16[128,3072]{1,0:T(8,128)(2,1)}, bf16[128,3072]{1,0:T(8,128)(2,1)}, u32[]{:S(2)}, u32[]{:S(2)}) collective-permute-start(bf16[128,3072]{1,0:T(8,128)(2,1)} %bitcast.70), channel_id=1, source_target_pairs={{0,1},{1,2},{2,3},{3,0},{4,5},{5,6},{6,7},{7,4},{8,9},{9,10},{10,1... | collective-permute-start | bytes 2359304 | tf_op jit(solution)/shard_map/ppermute | solution.py:115
  348.6 34.1 %collective-permute-start.28 = (bf16[128,3072]{1,0:T(8,128)(2,1)S(1)}, bf16[128,3072]{1,0:T(8,128)(2,1)S(1)}, u32[]{:S(2)}, u32[]{:S(2)}) collective-permute-start(bf16[128,3072]{1,0:T(8,128)(2,1)S(1)} %collective-permute-done.27), channel_id=1, source_target_pairs={{0,1},{1,2},{2,3},{3,0},{4,5},{5,6},{6,7},{7,4},{8,9},{9,10},{10,1... | collective-permute-start | bytes 2359304 | tf_op jit(solution)/shard_map/ppermute | solution.py:115
  394.2 17.9 %collective-permute-start.37 = (bf16[128,3072]{1,0:T(8,128)(2,1)}, bf16[128,3072]{1,0:T(8,128)(2,1)S(1)}, u32[]{:S(2)}, u32[]{:S(2)}) collective-permute-start(bf16[128,3072]{1,0:T(8,128)(2,1)} %collective-permute-done.36), channel_id=1, source_target_pairs={{0,1},{1,2},{2,3},{3,0},{4,5},{5,6},{6,7},{7,4},{8,9},{9,10},{10,1... | collective-permute-start | bytes 2359304 | tf_op jit(solution)/shard_map/ppermute | solution.py:115
  396.5 41.4 %collective-permute-start.35 = (bf16[64,3072]{1,0:T(8,128)(2,1)}, bf16[64,3072]{1,0:T(8,128)(2,1)S(1)}, u32[]{:S(2)}, u32[]{:S(2)}) collective-permute-start(bf16[64,3072]{1,0:T(8,128)(2,1)} %get-tuple-element.10), channel_id=1, source_target_pairs={{0,8},{4,12},{8,0},{12,4},{16,24},{20,28},{24,16},{28,20},{1,9},{5... | collective-permute-start | bytes 1179656 | tf_op jit(solution)/shard_map/ppermute | solution.py:158
  414.5 23.9 %collective-permute-start.30 = (bf16[64,3072]{1,0:T(8,128)(2,1)}, bf16[64,3072]{1,0:T(8,128)(2,1)}, u32[]{:S(2)}, u32[]{:S(2)}) collective-permute-start(bf16[64,3072]{1,0:T(8,128)(2,1)} %get-tuple-element.6), channel_id=1, source_target_pairs={{0,20},{4,16},{8,28},{12,24},{16,4},{20,0},{24,12},{28,8},{1,21},{... | collective-permute-start | bytes 1179656 | tf_op jit(solution)/shard_map/ppermute | solution.py:158
  414.7 23.8 %collective-permute-start.34 = (bf16[64,3072]{1,0:T(8,128)(2,1)}, bf16[64,3072]{1,0:T(8,128)(2,1)}, u32[]{:S(2)}, u32[]{:S(2)}) collective-permute-start(bf16[64,3072]{1,0:T(8,128)(2,1)} %get-tuple-element.7), channel_id=1, source_target_pairs={{0,4},{4,0},{8,12},{12,8},{16,20},{20,16},{24,28},{28,24},{1,5},{5... | collective-permute-start | bytes 1179656 | tf_op jit(solution)/shard_map/ppermute | solution.py:158
  417.7 20.8 %collective-permute-start.32 = (bf16[64,3072]{1,0:T(8,128)(2,1)}, bf16[64,3072]{1,0:T(8,128)(2,1)}, u32[]{:S(2)}, u32[]{:S(2)}) collective-permute-start(bf16[64,3072]{1,0:T(8,128)(2,1)} %get-tuple-element.8), channel_id=1, source_target_pairs={{0,16},{4,20},{8,24},{12,28},{16,0},{20,4},{24,8},{28,12},{1,17},{... | collective-permute-start | bytes 1179656 | tf_op jit(solution)/shard_map/ppermute | solution.py:158
  440.1 34.3 %collective-permute-start.45 = (bf16[64,3072]{1,0:T(8,128)(2,1)S(1)}, bf16[64,3072]{1,0:T(8,128)(2,1)S(1)}, u32[]{:S(2)}, u32[]{:S(2)}) collective-permute-start(bf16[64,3072]{1,0:T(8,128)(2,1)S(1)} %get-tuple-element.17), channel_id=1, source_target_pairs={{0,8},{4,12},{8,0},{12,4},{16,24},{20,28},{24,16},{28,20},{1,9},{5... | collective-permute-start | bytes 1179656 | tf_op jit(solution)/shard_map/ppermute | solution.py:158
  441.1 33.3 %collective-permute-start.40 = (bf16[64,3072]{1,0:T(8,128)(2,1)S(1)}, bf16[64,3072]{1,0:T(8,128)(2,1)S(1)}, u32[]{:S(2)}, u32[]{:S(2)}) collective-permute-start(bf16[64,3072]{1,0:T(8,128)(2,1)S(1)} %get-tuple-element.13), channel_id=1, source_target_pairs={{0,20},{4,16},{8,28},{12,24},{16,4},{20,0},{24,12},{28,8},{1,21},{... | collective-permute-start | bytes 1179656 | tf_op jit(solution)/shard_map/ppermute | solution.py:158
  441.2 33.2 %collective-permute-start.44 = (bf16[64,3072]{1,0:T(8,128)(2,1)S(1)}, bf16[64,3072]{1,0:T(8,128)(2,1)S(1)}, u32[]{:S(2)}, u32[]{:S(2)}) collective-permute-start(bf16[64,3072]{1,0:T(8,128)(2,1)S(1)} %get-tuple-element.14), channel_id=1, source_target_pairs={{0,4},{4,0},{8,12},{12,8},{16,20},{20,16},{24,28},{28,24},{1,5},{5... | collective-permute-start | bytes 1179656 | tf_op jit(solution)/shard_map/ppermute | solution.py:158
  444.5 29.9 %collective-permute-start.42 = (bf16[64,3072]{1,0:T(8,128)(2,1)S(1)}, bf16[64,3072]{1,0:T(8,128)(2,1)S(1)}, u32[]{:S(2)}, u32[]{:S(2)}) collective-permute-start(bf16[64,3072]{1,0:T(8,128)(2,1)S(1)} %get-tuple-element.15), channel_id=1, source_target_pairs={{0,16},{4,20},{8,24},{12,28},{16,0},{20,4},{24,8},{28,12},{1,17},{... | collective-permute-start | bytes 1179656 | tf_op jit(solution)/shard_map/ppermute | solution.py:158
  (35 other events, 641.8 us)
Sparse Core Ops, SparseCore 0:
  67.7 45.7 all-gather.1
  295.2 61.9 reduce-scatter.1

commit v3 on v2

--- a/solution.py
+++ b/solution.py
@@ -93,7 +93,7 @@
 def qkv_weight_grad(tokens_parts, grads_parts, heads, head):
     count, width = tokens_parts[0].shape
     columns = grads_parts[0].shape[1]
-    block = 256
+    block = 512
     rows = pl.pallas_call(
         functools.partial(qkv_weight_kernel, heads, head),
         grid=(width // block,),
@@ -115,17 +115,21 @@
     return lax.ppermute(block, "depth", [(i, (i + 1) % size) for i in range(size)])
 
 
-def ring_sum(partial, size):
+def ring_sum(partial, size, before_last=()):
     me = lax.axis_index("depth")
 
     def chunk(back):
         return lax.dynamic_index_in_dim(partial, lax.rem(me + 2 * size - back, size), 0, False)
 
     running = chunk(1).astype(jnp.bfloat16)
+    sums = []
     for step in range(1, size):
+        if step == size - 1:
+            running = after(running, *before_last)
         arrived = send_on(running, size).astype(jnp.float32)
         running = (arrived + chunk(1 + step)).astype(jnp.bfloat16)
-    return running
+        sums.append(running)
+    return running, sums[0]
 
 
 def ring_gather(block, size):
@@ -158,18 +162,6 @@
     return lax.ppermute(block, ("row", "col"), [(i, i ^ mask) for i in range(group)])
 
 
-def gather_direct(block, group, core):
-    me = lax.axis_index(("row", "col"))
-    masks = [m for m in range(group) if not m & core]
-    out = jnp.zeros((group,) + block.shape, block.dtype)
-    from_chips = [swap(block, m, group) if m else block for m in masks]
-    for mask, arrived in zip(masks, from_chips):
-        out = lax.dynamic_update_index_in_dim(out, arrived, me ^ mask, 0)
-        other = swap(arrived, core, group)
-        out = lax.dynamic_update_index_in_dim(out, other, me ^ (mask | core), 0)
-    return out.reshape(group * block.shape[0], block.shape[1]), from_chips[-1]
-
-
 def scatter_direct(whole, group, core):
     me = lax.axis_index(("row", "col"))
     masks = [m for m in range(group) if not m & core]
@@ -199,33 +191,31 @@
     qkv_flat = w_qkv.reshape(width, columns)
     out_flat = w_out.reshape(hidden, width)
 
-    gathered = []
-    last_arrival = None
-    for p in range(PIECES):
-        part = tokens[p * part_rows : (p + 1) * part_rows]
-        part = part if last_arrival is None else after(part, last_arrival)
-        whole, last_arrival = gather_direct(part, group, core)
-        gathered.append(whole)
+    gathered = [
+        gather_rows(tokens[p * part_rows : (p + 1) * part_rows]) for p in range(PIECES)
+    ]
+    grad_all = gather_rows(after(d_output, gathered[-1]))
+    d_mixed_terms = dot_f32(grad_all, out_flat, CONTRACT_LAST)
+
     pieces = []
-    for piece in gathered:
-        partial = dot_f32(piece, qkv_flat)
-        pieces.append(ring_sum(partial.reshape(size, sharers * part_rows, columns), size))
+    for p, piece in enumerate(gathered):
+        partial = dot_f32(piece, qkv_flat).reshape(size, sharers * part_rows, columns)
+        before_last = (d_mixed_terms,) if p == PIECES - 1 else ()
+        pieces.append(ring_sum(partial, size, before_last)[0])
+    d_mixed, d_mixed_first = ring_sum(d_mixed_terms.reshape(size, seq_len, hidden), size)
+
     projected = jnp.stack([p.reshape(sharers, part_rows, columns) for p in pieces], axis=1)
-    projected = projected.reshape(seq_len, columns)
-
-    grad_all = gather_rows(after(d_output, last_arrival))
-    d_mixed = dot_f32(grad_all, out_flat, CONTRACT_LAST)
-    d_mixed = ring_sum(d_mixed.reshape(size, seq_len, hidden), size)
+    projected = after(projected.reshape(seq_len, columns), d_mixed_first)
 
     mixed = attention_call(attend_kernel, positions, head, heads, False, projected)
     heads_all, mixed_arrivals = ring_gather(mixed, size)
     heads_all = heads_all.reshape(size * seq_len, hidden)
-    output_terms = dot_f32(heads_all, out_flat).astype(jnp.bfloat16)
-    output = scatter_rows(output_terms)
-
     grads = attention_call(
         attend_back_kernel, positions, head, heads, True, projected, after(d_mixed, mixed_arrivals[-1])
     )
+    heads_all = after(heads_all, grads)
+    output_terms = dot_f32(heads_all, out_flat).astype(jnp.bfloat16)
+    output = scatter_rows(output_terms)
     d_out_weight = dot_f32(heads_all, grad_all, CONTRACT_FIRST)
 
     grads = grads.reshape(sharers, PIECES, part_rows, columns)
@@ -234,7 +224,7 @@
     arrivals = None
     for p in range(PIECES):
         own = grads[:, p].reshape(sharers * part_rows, columns)
-        own = own if arrivals is None else after(own, arrivals[-2], output_terms)
+        own = own if arrivals is None else after(own, arrivals[-1], output_terms)
         piece, arrivals = ring_gather(own, size)
         piece = piece.reshape(size * sharers * part_rows, columns)
         all_grads.append(piece)

time: 485 us -> 472 us (0.973)
  local copies, waits for them, and re-layouts: 67 us -> 44.7 us
  waiting for transfers between devices: 218 us -> 234 us
  starting transfers between devices: 23.7 us -> 17.1 us
    all_gather x1 -> x3, waiting for transfers between devices: 0.01 us -> 41.6 us  [gather_rows(): return lax.all_gather(local_rows, ('row', 'col'), axis=0, tiled=True)]
    dynamic_update_slice x15 -> x0, local copies, waits for them, and re-layouts: 14.8 us -> none  [the longest x7 8.56 us: gather_direct(): out = lax.dynamic_update_index_in_dim(out, arrived, me ^ mask, 0)]
    ppermute x28 -> x14, waiting for transfers between devices: 16 us -> 1.52 us  [swap(): lax.ppermute(block, ('row', 'col'), [(i, i ^ mask) for i in range(group)])]
    ppermute x18, waiting for transfers between devices: 202 us -> 190 us  [send_on(): lax.ppermute(block, 'depth', [(i, (i + 1) % size) for i in range(size)])]
    ppermute x28 -> x14, starting transfers between devices: 18.4 us -> 9.33 us  [swap(): lax.ppermute(block, ('row', 'col'), [(i, i ^ mask) for i in range(group)])]
    unnamed x39 -> x33, local copies, waits for them, and re-layouts: 31.3 us -> 28.4 us
    convert_element_type x8 -> x7, other arithmetic: 12.5 us -> 11.5 us  [ring_sum(): running = (arrived + chunk(1 + step)).astype(jnp.bfloat16)]
  transfers between devices with their start and end apart: 48 -> 36, of which waited for: 17 -> 22; matrix products, arithmetic and copies ran while one was open for 35% -> 30% of each run, Pallas kernels for 9% -> 6%
where the time goes in v3:
time: 472 us; the launch traced here: 471 us
  waiting for transfers between devices  234 us (50%)
  matrix products  89.4 us (19%)
  Pallas kernels  45.3 us (10%)
  local copies, waits for them, and re-layouts  44.7 us (9%)
  other arithmetic  20.6 us (4%)
  between operations  19.6 us (4%)
  starting transfers between devices  17.1 us (4%)
    ppermute x18, waiting for transfers between devices, send_on(): lax.ppermute(block, 'depth', [(i, (i + 1) % size) for i in range(size)])  190 us
    dot_general x7, matrix products, dot_f32(): lax.dot_general(left, right, dims, preferred_element_type=jnp.float32)  89.4 us
    all_gather x3, waiting for transfers between devices, gather_rows(): return lax.all_gather(local_rows, ('row', 'col'), axis=0, tiled=True)  41.6 us
    pallas_call x1, Pallas kernels, qkv_weight_grad(): pl.pallas_call(functools.partial(qkv_weight_kernel, heads, head), grid=(w...  30 us
    unnamed x33, local copies, waits for them, and re-layouts  28.4 us
    pallas_call x2, Pallas kernels, attention_call(): pl.pallas_call(functools.partial(kernel, score_scale, head), grid=(heads,...  15.3 us
    convert_element_type x7, other arithmetic, ring_sum(): running = (arrived + chunk(1 + step)).astype(jnp.bfloat16)  11.5 us
  transfers between devices with their start and end apart: 36, of which 22 were waited for; matrix products, arithmetic and copies ran while one was open for 30% of the time, Pallas kernels for 6%

profile of v3, /device:TPU:0, one launch (start us, length us, event | category | flops | bytes accessed | tf_op | source)
XLA Modules:
  0.0 470.9 jit_solution(8803116860975577136)
XLA Ops:
  10.1 35.4 %all-gather.6.cloned.1.call-done.refs_1_ = bf16[512,3072]{1,0:T(8,128)(2,1)} async-done(((bf16[64,3072]{1,0:T(8,128)(2,1)}), bf16[512,3072]{1,0:T(8,128)(2,1)}) %all-gather.6.cloned.1.call-update) | async-done | bytes 3145744 | tf_op jit(solution)/shard_map/all_gather | solution.py:154
  49.5 24.6 %copy.12 = bf16[3072,8,3,128]{0,3,2,1:T(8,128)(2,1)} copy(bf16[3072,8,3,128]{3,1,2,0:T(8,128)(2,1)} %param.6) | data formatting | bytes 37748736 | tf_op args[1]
  74.1 6.2 %all-gather.4.cloned.1.call-done.refs_0_ = bf16[512,3072]{1,0:T(8,128)(2,1)} async-done(((bf16[64,3072]{1,0:T(8,128)(2,1)}), bf16[512,3072]{1,0:T(8,128)(2,1)}) %all-gather.4.cloned.1.call-update) | async-done | bytes 3145744 | tf_op jit(solution)/shard_map/all_gather | solution.py:154
  80.3 14.1 %fusion.28 = f32[4,128,3072]{2,1,0:T(8,128)S(1)} fusion(bf16[4,128,3072]{2,1,0:T(8,128)(2,1)} %bitcast.199, bf16[3072,3072,1]{0,1,2:T(8,128)(2,1)} %bitcast.161), kind=kOutput, calls=%fused_computation.76 | convolution fusion | flops 9663676416 | bytes 28311552 | tf_op jit(solution)/shard_map/dot_general | solution.py:18
  97.1 14.1 %fusion.29 = f32[4,128,3072]{2,1,0:T(8,128)S(1)} fusion(bf16[4,128,3072]{2,1,0:T(8,128)(2,1)} %bitcast.198, bf16[3072,3072,1]{0,1,2:T(8,128)(2,1)} %bitcast.162), kind=kOutput, calls=%fused_computation.77 | convolution fusion | flops 9663676416 | bytes 28311552 | tf_op jit(solution)/shard_map/dot_general | solution.py:18
  111.2 2.7 copy-done.1
  116.2 2.7 fusion.7
  120.5 15.7 %collective-permute-done.3 = bf16[128,3072]{1,0:T(8,128)(2,1)S(1)} collective-permute-done((bf16[128,3072]{1,0:T(8,128)(2,1)S(1)}, bf16[128,3072]{1,0:T(8,128)(2,1)S(1)}, u32[]{:S(2)}, u32[]{:S(2)}) %collective-permute-start.3) | collective-permute-done | bytes 786464 | tf_op jit(solution)/shard_map/ppermute | solution.py:115
  136.2 2.4 fusion.4
  138.6 14.5 %collective-permute-done.1 = bf16[128,3072]{1,0:T(8,128)(2,1)} collective-permute-done((bf16[128,3072]{1,0:T(8,128)(2,1)}, bf16[128,3072]{1,0:T(8,128)(2,1)}, u32[]{:S(2)}, u32[]{:S(2)}) %collective-permute-start.1) | collective-permute-done | bytes 786464 | tf_op jit(solution)/shard_map/ppermute | solution.py:115
  153.2 2.8 fusion.6
  156.0 10.8 %fusion.30 = f32[1024,1024]{1,0:T(8,128)S(1)} fusion(bf16[1024,3072]{1,0:T(8,128)(2,1)} %all-gather.8.cloned.1.call-done, bf16[1024,3072]{1,0:T(8,128)(2,1)} %bitcast.196), kind=kOutput, calls=%fused_computation.78 | convolution fusion | flops 6442450944 | bytes 16777216 | tf_op jit(solution)/shard_map/dot_general | solution.py:18
  171.3 15.6 %collective-permute-done.2 = bf16[128,3072]{1,0:T(8,128)(2,1)} collective-permute-done((bf16[128,3072]{1,0:T(8,128)(2,1)}, bf16[128,3072]{1,0:T(8,128)(2,1)}, u32[]{:S(2)}, u32[]{:S(2)}) %collective-permute-start.2) | collective-permute-done | bytes 786464 | tf_op jit(solution)/shard_map/ppermute | solution.py:115
  188.7 9.3 %collective-permute-done.6 = bf16[256,1024]{1,0:T(8,128)(2,1)S(1)} collective-permute-done((bf16[256,1024]{1,0:T(8,128)(2,1)S(1)}, bf16[256,1024]{1,0:T(8,128)(2,1)S(1)}, u32[]{:S(2)}, u32[]{:S(2)}) %collective-permute-start.6) | collective-permute-done | bytes 524320 | tf_op jit(solution)/shard_map/ppermute | solution.py:115
  199.3 14.8 %collective-permute-done.5 = bf16[128,3072]{1,0:T(8,128)(2,1)S(1)} collective-permute-done((bf16[128,3072]{1,0:T(8,128)(2,1)S(1)}, bf16[128,3072]{1,0:T(8,128)(2,1)S(1)}, u32[]{:S(2)}, u32[]{:S(2)}) %collective-permute-start.5) | collective-permute-done | bytes 786464 | tf_op jit(solution)/shard_map/ppermute | solution.py:115
  215.7 7.0 %shard_map.84 = bf16[256,1024]{1,0:T(8,128)(2,1)} custom-call(s32[256,1]{1,0:T(8,128)} %copy.17.positions_ref, bf16[256,3072]{1,0:T(8,128)(2,1)} %bitcast.167), custom_call_target="tpu_custom_call" | custom-call | flops 268435456 | bytes 2097152 | tf_op jit(solution)/shard_map/pallas_call | solution.py:63
  223.9 15.7 %collective-permute-done.7 = bf16[256,1024]{1,0:T(8,128)(2,1)S(1)} collective-permute-done((bf16[256,1024]{1,0:T(8,128)(2,1)}, bf16[256,1024]{1,0:T(8,128)(2,1)S(1)}, u32[]{:S(2)}, u32[]{:S(2)}) %collective-permute-start.7) | collective-permute-done | bytes 524320 | tf_op jit(solution)/shard_map/ppermute | solution.py:115
  239.6 11.2 %collective-permute-done.10 = bf16[256,1024]{1,0:T(8,128)(2,1)S(1)} collective-permute-done((bf16[256,1024]{1,0:T(8,128)(2,1)S(1)}, bf16[256,1024]{1,0:T(8,128)(2,1)S(1)}, u32[]{:S(2)}, u32[]{:S(2)}) %collective-permute-start.10) | collective-permute-done | bytes 524320 | tf_op jit(solution)/shard_map/ppermute | solution.py:115
  252.2 9.8 %collective-permute-done.8 = bf16[256,1024]{1,0:T(8,128)(2,1)S(1)} collective-permute-done((bf16[256,1024]{1,0:T(8,128)(2,1)S(1)}, bf16[256,1024]{1,0:T(8,128)(2,1)S(1)}, u32[]{:S(2)}, u32[]{:S(2)}) %collective-permute-start.8) | collective-permute-done | bytes 524320 | tf_op jit(solution)/shard_map/ppermute | solution.py:115
  262.4 20.5 %collective-permute-done.9 = bf16[256,1024]{1,0:T(8,128)(2,1)S(1)} collective-permute-done((bf16[256,1024]{1,0:T(8,128)(2,1)S(1)}, bf16[256,1024]{1,0:T(8,128)(2,1)S(1)}, u32[]{:S(2)}, u32[]{:S(2)}) %collective-permute-start.9) | collective-permute-done | bytes 524320 | tf_op jit(solution)/shard_map/ppermute | solution.py:115
  286.3 8.3 %shard_map.85 = bf16[256,3072]{1,0:T(8,128)(2,1)} custom-call(s32[256,1]{1,0:T(8,128)} %copy.17.positions_ref, bf16[256,3072]{1,0:T(8,128)(2,1)} %bitcast.168, bf16[256,1024]{1,0:T(8,128)(2,1)} %fusion.26.d_mixed_ref), custom_call_target="tpu_custom_call" | custom-call | flops 939524096 | bytes 6291456 | tf_op jit(solution)/shard_map/pallas_call | solution.py:63
  297.9 11.4 %convolution_convert_fusion = bf16[1024,3072]{1,0:T(8,128)(2,1)} fusion(bf16[1024,1024]{1,0:T(8,128)(2,1)S(1)} %bitcast.193, bf16[1024,3072]{1,0:T(8,128)(2,1)} %bitcast.197), kind=kOutput, calls=%fused_computation | convolution fusion | flops 6445596672 | bytes 14680064 | tf_op jit(solution)/shard_map/dot_general | solution.py:18
  309.3 8.3 %collective-permute-done.12 = bf16[128,3072]{1,0:T(8,128)(2,1)} collective-permute-done((bf16[128,3072]{1,0:T(8,128)(2,1)S(1)}, bf16[128,3072]{1,0:T(8,128)(2,1)}, u32[]{:S(2)}, u32[]{:S(2)}) %collective-permute-start.12) | collective-permute-done | bytes 786464 | tf_op jit(solution)/shard_map/ppermute | solution.py:115
  317.6 12.7 %fusion.31 = f32[1024,3072]{1,0:T(8,128)} fusion(bf16[1024,1024]{1,0:T(8,128)(2,1)S(1)} %bitcast.194, bf16[1024,3072]{1,0:T(8,128)(2,1)} %all-gather.8.cloned.1.call-done), kind=kOutput, calls=%fused_computation.79 | convolution fusion | flops 6442450944 | bytes 20971520 | tf_op jit(solution)/shard_map/dot_general | solution.py:18
  334.4 2.2 collective-permute-done.13
  337.9 16.6 %collective-permute-done.14 = bf16[128,3072]{1,0:T(8,128)(2,1)S(1)} collective-permute-done((bf16[128,3072]{1,0:T(8,128)(2,1)S(1)}, bf16[128,3072]{1,0:T(8,128)(2,1)S(1)}, u32[]{:S(2)}, u32[]{:S(2)}) %collective-permute-start.14) | collective-permute-done | bytes 786464 | tf_op jit(solution)/shard_map/ppermute | solution.py:115
  356.0 11.4 %fusion = bf16[512,3072]{1,0:T(8,128)(2,1)} fusion(bf16[512,3072]{1,0:T(8,128)(2,1)S(1)} %bitcast.181, bf16[3072,3072]{0,1:T(8,128)(2,1)S(1)} %bitcast.166, bf16[]{:T(256)} %bitcast.42), kind=kOutput, calls=%fused_computation.3 | convolution fusion | flops 9666822144 | bytes 25165826 | tf_op jit(solution)/shard_map/dot_general | solution.py:18
  367.4 2.2 dynamic-slice_bitcast_fusion.7
  378.2 14.1 %collective-permute-done.23 = bf16[128,3072]{1,0:T(8,128)(2,1)S(1)} collective-permute-done((bf16[128,3072]{1,0:T(8,128)(2,1)S(1)}, bf16[128,3072]{1,0:T(8,128)(2,1)S(1)}, u32[]{:S(2)}, u32[]{:S(2)}) %collective-permute-start.23) | collective-permute-done | bytes 786464 | tf_op jit(solution)/shard_map/ppermute | solution.py:115
  392.5 18.5 %collective-permute-done.24 = bf16[128,3072]{1,0:T(8,128)(2,1)S(1)} collective-permute-done((bf16[128,3072]{1,0:T(8,128)(2,1)S(1)}, bf16[128,3072]{1,0:T(8,128)(2,1)S(1)}, u32[]{:S(2)}, u32[]{:S(2)}) %collective-permute-start.24) | collective-permute-done | bytes 786464 | tf_op jit(solution)/shard_map/ppermute | solution.py:115
  411.1 15.0 %fusion.1 = bf16[512,3072]{1,0:T(8,128)(2,1)S(1)} fusion(bf16[512,3072]{1,0:T(8,128)(2,1)S(1)} %bitcast.179, bf16[3072,3072]{0,1:T(8,128)(2,1)} %bitcast.163, bf16[]{:T(256)} %bitcast.42), kind=kOutput, calls=%fused_computation.4 | convolution fusion | flops 9666822144 | bytes 25165826 | tf_op jit(solution)/shard_map/dot_general | solution.py:18
  433.1 30.0 %shard_map.86 = f32[73728,128]{1,0:T(8,128)} custom-call(bf16[512,3072]{1,0:T(8,128)(2,1)} %all-gather.4.cloned.1.call-done.refs_0_, bf16[512,3072]{1,0:T(8,128)(2,1)} %all-gather.6.cloned.1.call-done.refs_1_, bf16[512,3072]{1,0:T(8,128)(2,1)} %bitcast.182, bf16[512,3072]{1,0:T(8,128)(2,1)} %bitcast.180), custom_call_target="tpu_custom_call" | custom-call | flops 19327352832 | bytes 50331648 | tf_op jit(solution)/shard_map/pallas_call | solution.py:97
  (138 shorter events, 50.6 us)
Async XLA Ops:
  7.2 38.3 %all-gather.6.cloned.1.call-start = ((), (), s32[]{:S(2)}) async-start(), calls=%async_computation.2 | async-start | bytes 3538944 | tf_op jit(solution)/shard_map/all_gather | solution.py:154
  9.3 71.0 %all-gather.4.cloned.1.call-start = ((), (), s32[]{:S(2)}) async-start(), calls=%async_computation.1 | async-start | bytes 3538944 | tf_op jit(solution)/shard_map/all_gather | solution.py:154
  10.0 145.9 %all-gather.8.cloned.1.call-start = ((), (), s32[]{:S(2)}) async-start(), calls=%async_computation.3 | async-start | bytes 7077888 | tf_op jit(solution)/shard_map/all_gather | solution.py:154
  49.4 414.9 %reduce-scatter.2.cloned.1.call-start = ((), (), s32[]{:S(2)}) async-start(), calls=%async_computation.4 | async-start | bytes 7077888 | tf_op jit(solution)/shard_map/reduce_scatter | solution.py:158
  94.5 21.7 %collective-permute-start = (bf16[128,3072]{1,0:T(8,128)(2,1)S(1)}, bf16[128,3072]{1,0:T(8,128)(2,1)}, u32[]{:S(2)}, u32[]{:S(2)}) collective-permute-start(bf16[128,3072]{1,0:T(8,128)(2,1)S(1)} %fusion.11), channel_id=1, source_target_pairs={{0,1},{1,2},{2,3},{3,0},{4,5},{5,6},{6,7},{7,4},{8,9},{9,10},{10,1... | collective-permute-start | bytes 2359304 | tf_op jit(solution)/shard_map/ppermute | solution.py:115
  114.0 22.2 %collective-permute-start.3 = (bf16[128,3072]{1,0:T(8,128)(2,1)S(1)}, bf16[128,3072]{1,0:T(8,128)(2,1)S(1)}, u32[]{:S(2)}, u32[]{:S(2)}) collective-permute-start(bf16[128,3072]{1,0:T(8,128)(2,1)S(1)} %fusion.12), channel_id=1, source_target_pairs={{0,1},{1,2},{2,3},{3,0},{4,5},{5,6},{6,7},{7,4},{8,9},{9,10},{10,1... | collective-permute-start | bytes 2359304 | tf_op jit(solution)/shard_map/ppermute | solution.py:115
  118.9 34.3 %collective-permute-start.1 = (bf16[128,3072]{1,0:T(8,128)(2,1)}, bf16[128,3072]{1,0:T(8,128)(2,1)}, u32[]{:S(2)}, u32[]{:S(2)}) collective-permute-start(bf16[128,3072]{1,0:T(8,128)(2,1)} %fusion.7), channel_id=1, source_target_pairs={{0,1},{1,2},{2,3},{3,0},{4,5},{5,6},{6,7},{7,4},{8,9},{9,10},{10,1... | collective-permute-start | bytes 2359304 | tf_op jit(solution)/shard_map/ppermute | solution.py:115
  138.6 31.3 %collective-permute-start.4 = (bf16[128,3072]{1,0:T(8,128)(2,1)}, bf16[128,3072]{1,0:T(8,128)(2,1)S(1)}, u32[]{:S(2)}, u32[]{:S(2)}) collective-permute-start(bf16[128,3072]{1,0:T(8,128)(2,1)} %fusion.4), channel_id=1, source_target_pairs={{0,1},{1,2},{2,3},{3,0},{4,5},{5,6},{6,7},{7,4},{8,9},{9,10},{10,1... | collective-permute-start | bytes 2359304 | tf_op jit(solution)/shard_map/ppermute | solution.py:115
  156.0 30.9 %collective-permute-start.2 = (bf16[128,3072]{1,0:T(8,128)(2,1)}, bf16[128,3072]{1,0:T(8,128)(2,1)}, u32[]{:S(2)}, u32[]{:S(2)}) collective-permute-start(bf16[128,3072]{1,0:T(8,128)(2,1)} %fusion.6), channel_id=1, source_target_pairs={{0,1},{1,2},{2,3},{3,0},{4,5},{5,6},{6,7},{7,4},{8,9},{9,10},{10,1... | collective-permute-start | bytes 2359304 | tf_op jit(solution)/shard_map/ppermute | solution.py:115
  167.4 30.6 %collective-permute-start.6 = (bf16[256,1024]{1,0:T(8,128)(2,1)S(1)}, bf16[256,1024]{1,0:T(8,128)(2,1)S(1)}, u32[]{:S(2)}, u32[]{:S(2)}) collective-permute-start(bf16[256,1024]{1,0:T(8,128)(2,1)S(1)} %fusion.25), channel_id=1, source_target_pairs={{0,1},{1,2},{2,3},{3,0},{4,5},{5,6},{6,7},{7,4},{8,9},{9,10},{10,1... | collective-permute-start | bytes 1572872 | tf_op jit(solution)/shard_map/ppermute | solution.py:115
  170.1 44.1 %collective-permute-start.5 = (bf16[128,3072]{1,0:T(8,128)(2,1)S(1)}, bf16[128,3072]{1,0:T(8,128)(2,1)S(1)}, u32[]{:S(2)}, u32[]{:S(2)}) collective-permute-start(bf16[128,3072]{1,0:T(8,128)(2,1)S(1)} %fusion.13), channel_id=1, source_target_pairs={{0,1},{1,2},{2,3},{3,0},{4,5},{5,6},{6,7},{7,4},{8,9},{9,10},{10,1... | collective-permute-start | bytes 2359304 | tf_op jit(solution)/shard_map/ppermute | solution.py:115
  222.7 16.9 %collective-permute-start.7 = (bf16[256,1024]{1,0:T(8,128)(2,1)}, bf16[256,1024]{1,0:T(8,128)(2,1)S(1)}, u32[]{:S(2)}, u32[]{:S(2)}) collective-permute-start(bf16[256,1024]{1,0:T(8,128)(2,1)} %shard_map.84), channel_id=1, source_target_pairs={{0,1},{1,2},{2,3},{3,0},{4,5},{5,6},{6,7},{7,4},{8,9},{9,10},{10,1... | collective-permute-start | bytes 1572872 | tf_op jit(solution)/shard_map/ppermute | solution.py:115
  222.7 28.1 %collective-permute-start.10 = (bf16[256,1024]{1,0:T(8,128)(2,1)S(1)}, bf16[256,1024]{1,0:T(8,128)(2,1)S(1)}, u32[]{:S(2)}, u32[]{:S(2)}) collective-permute-start(bf16[256,1024]{1,0:T(8,128)(2,1)S(1)} %fusion.10), channel_id=1, source_target_pairs={{0,1},{1,2},{2,3},{3,0},{4,5},{5,6},{6,7},{7,4},{8,9},{9,10},{10,1... | collective-permute-start | bytes 1572872 | tf_op jit(solution)/shard_map/ppermute | solution.py:115
  239.6 22.5 %collective-permute-start.8 = (bf16[256,1024]{1,0:T(8,128)(2,1)S(1)}, bf16[256,1024]{1,0:T(8,128)(2,1)S(1)}, u32[]{:S(2)}, u32[]{:S(2)}) collective-permute-start(bf16[256,1024]{1,0:T(8,128)(2,1)S(1)} %collective-permute-done.7), channel_id=1, source_target_pairs={{0,1},{1,2},{2,3},{3,0},{4,5},{5,6},{6,7},{7,4},{8,9},{9,10},{10,1... | collective-permute-start | bytes 1572872 | tf_op jit(solution)/shard_map/ppermute | solution.py:115
  252.2 31.9 %collective-permute-start.11 = (bf16[256,1024]{1,0:T(8,128)(2,1)S(1)}, bf16[256,1024]{1,0:T(8,128)(2,1)S(1)}, u32[]{:S(2)}, u32[]{:S(2)}) collective-permute-start(bf16[256,1024]{1,0:T(8,128)(2,1)S(1)} %fusion.9), channel_id=1, source_target_pairs={{0,1},{1,2},{2,3},{3,0},{4,5},{5,6},{6,7},{7,4},{8,9},{9,10},{10,1... | collective-permute-start | bytes 1572872 | tf_op jit(solution)/shard_map/ppermute | solution.py:115
  262.0 20.9 %collective-permute-start.9 = (bf16[256,1024]{1,0:T(8,128)(2,1)S(1)}, bf16[256,1024]{1,0:T(8,128)(2,1)S(1)}, u32[]{:S(2)}, u32[]{:S(2)}) collective-permute-start(bf16[256,1024]{1,0:T(8,128)(2,1)S(1)} %collective-permute-done.8), channel_id=1, source_target_pairs={{0,1},{1,2},{2,3},{3,0},{4,5},{5,6},{6,7},{7,4},{8,9},{9,10},{10,1... | collective-permute-start | bytes 1572872 | tf_op jit(solution)/shard_map/ppermute | solution.py:115
  297.6 19.9 %collective-permute-start.12 = (bf16[128,3072]{1,0:T(8,128)(2,1)S(1)}, bf16[128,3072]{1,0:T(8,128)(2,1)}, u32[]{:S(2)}, u32[]{:S(2)}) collective-permute-start(bf16[128,3072]{1,0:T(8,128)(2,1)S(1)} %bitcast.177), channel_id=1, source_target_pairs={{0,1},{1,2},{2,3},{3,0},{4,5},{5,6},{6,7},{7,4},{8,9},{9,10},{10,1... | collective-permute-start | bytes 2359304 | tf_op jit(solution)/shard_map/ppermute | solution.py:115
  317.5 19.0 %collective-permute-start.13 = (bf16[128,3072]{1,0:T(8,128)(2,1)}, bf16[128,3072]{1,0:T(8,128)(2,1)S(1)}, u32[]{:S(2)}, u32[]{:S(2)}) collective-permute-start(bf16[128,3072]{1,0:T(8,128)(2,1)} %collective-permute-done.12), channel_id=1, source_target_pairs={{0,1},{1,2},{2,3},{3,0},{4,5},{5,6},{6,7},{7,4},{8,9},{9,10},{10,1... | collective-permute-start | bytes 2359304 | tf_op jit(solution)/shard_map/ppermute | solution.py:115
  336.6 17.9 %collective-permute-start.14 = (bf16[128,3072]{1,0:T(8,128)(2,1)S(1)}, bf16[128,3072]{1,0:T(8,128)(2,1)S(1)}, u32[]{:S(2)}, u32[]{:S(2)}) collective-permute-start(bf16[128,3072]{1,0:T(8,128)(2,1)S(1)} %collective-permute-done.13), channel_id=1, source_target_pairs={{0,1},{1,2},{2,3},{3,0},{4,5},{5,6},{6,7},{7,4},{8,9},{9,10},{10,1... | collective-permute-start | bytes 2359304 | tf_op jit(solution)/shard_map/ppermute | solution.py:115
  355.7 17.0 %collective-permute-start.22 = (bf16[128,3072]{1,0:T(8,128)(2,1)S(1)}, bf16[128,3072]{1,0:T(8,128)(2,1)S(1)}, u32[]{:S(2)}, u32[]{:S(2)}) collective-permute-start(bf16[128,3072]{1,0:T(8,128)(2,1)S(1)} %bitcast.183), channel_id=1, source_target_pairs={{0,1},{1,2},{2,3},{3,0},{4,5},{5,6},{6,7},{7,4},{8,9},{9,10},{10,1... | collective-permute-start | bytes 2359304 | tf_op jit(solution)/shard_map/ppermute | solution.py:115
  369.6 3.7 collective-permute-start.15
  369.6 3.7 collective-permute-start.19
  370.1 56.1 %collective-permute-start.21 = (bf16[64,3072]{1,0:T(8,128)(2,1)S(1)}, bf16[64,3072]{1,0:T(8,128)(2,1)S(1)}, u32[]{:S(2)}, u32[]{:S(2)}) collective-permute-start(bf16[64,3072]{1,0:T(8,128)(2,1)S(1)} %get-tuple-element.8), channel_id=1, source_target_pairs={{0,8},{4,12},{8,0},{12,4},{16,24},{20,28},{24,16},{28,20},{1,9},{5... | collective-permute-start | bytes 1179656 | tf_op jit(solution)/shard_map/ppermute | solution.py:162
  372.8 19.5 %collective-permute-start.23 = (bf16[128,3072]{1,0:T(8,128)(2,1)S(1)}, bf16[128,3072]{1,0:T(8,128)(2,1)S(1)}, u32[]{:S(2)}, u32[]{:S(2)}) collective-permute-start(bf16[128,3072]{1,0:T(8,128)(2,1)S(1)} %collective-permute-done.22), channel_id=1, source_target_pairs={{0,1},{1,2},{2,3},{3,0},{4,5},{5,6},{6,7},{7,4},{8,9},{9,10},{10,1... | collective-permute-start | bytes 2359304 | tf_op jit(solution)/shard_map/ppermute | solution.py:115
  374.7 52.1 %collective-permute-start.16 = (bf16[64,3072]{1,0:T(8,128)(2,1)S(1)}, bf16[64,3072]{1,0:T(8,128)(2,1)S(1)}, u32[]{:S(2)}, u32[]{:S(2)}) collective-permute-start(bf16[64,3072]{1,0:T(8,128)(2,1)S(1)} %get-tuple-element.4), channel_id=1, source_target_pairs={{0,20},{4,16},{8,28},{12,24},{16,4},{20,0},{24,12},{28,8},{1,21},{... | collective-permute-start | bytes 1179656 | tf_op jit(solution)/shard_map/ppermute | solution.py:162
  376.3 50.6 %collective-permute-start.20 = (bf16[64,3072]{1,0:T(8,128)(2,1)S(1)}, bf16[64,3072]{1,0:T(8,128)(2,1)S(1)}, u32[]{:S(2)}, u32[]{:S(2)}) collective-permute-start(bf16[64,3072]{1,0:T(8,128)(2,1)S(1)} %get-tuple-element.5), channel_id=1, source_target_pairs={{0,4},{4,0},{8,12},{12,8},{16,20},{20,16},{24,28},{28,24},{1,5},{5... | collective-permute-start | bytes 1179656 | tf_op jit(solution)/shard_map/ppermute | solution.py:162
  377.8 49.1 %collective-permute-start.18 = (bf16[64,3072]{1,0:T(8,128)(2,1)S(1)}, bf16[64,3072]{1,0:T(8,128)(2,1)S(1)}, u32[]{:S(2)}, u32[]{:S(2)}) collective-permute-start(bf16[64,3072]{1,0:T(8,128)(2,1)S(1)} %get-tuple-element.6), channel_id=1, source_target_pairs={{0,16},{4,20},{8,24},{12,28},{16,0},{20,4},{24,8},{28,12},{1,17},{... | collective-permute-start | bytes 1179656 | tf_op jit(solution)/shard_map/ppermute | solution.py:162
  392.3 18.7 %collective-permute-start.24 = (bf16[128,3072]{1,0:T(8,128)(2,1)S(1)}, bf16[128,3072]{1,0:T(8,128)(2,1)S(1)}, u32[]{:S(2)}, u32[]{:S(2)}) collective-permute-start(bf16[128,3072]{1,0:T(8,128)(2,1)S(1)} %collective-permute-done.23), channel_id=1, source_target_pairs={{0,1},{1,2},{2,3},{3,0},{4,5},{5,6},{6,7},{7,4},{8,9},{9,10},{10,1... | collective-permute-start | bytes 2359304 | tf_op jit(solution)/shard_map/ppermute | solution.py:115
  427.1 36.0 %collective-permute-start.31 = (bf16[64,3072]{1,0:T(8,128)(2,1)S(1)}, bf16[64,3072]{1,0:T(8,128)(2,1)S(1)}, u32[]{:S(2)}, u32[]{:S(2)}) collective-permute-start(bf16[64,3072]{1,0:T(8,128)(2,1)S(1)} %get-tuple-element.15), channel_id=1, source_target_pairs={{0,8},{4,12},{8,0},{12,4},{16,24},{20,28},{24,16},{28,20},{1,9},{5... | collective-permute-start | bytes 1179656 | tf_op jit(solution)/shard_map/ppermute | solution.py:162
  429.5 33.6 %collective-permute-start.26 = (bf16[64,3072]{1,0:T(8,128)(2,1)S(1)}, bf16[64,3072]{1,0:T(8,128)(2,1)S(1)}, u32[]{:S(2)}, u32[]{:S(2)}) collective-permute-start(bf16[64,3072]{1,0:T(8,128)(2,1)S(1)} %get-tuple-element.11), channel_id=1, source_target_pairs={{0,20},{4,16},{8,28},{12,24},{16,4},{20,0},{24,12},{28,8},{1,21},{... | collective-permute-start | bytes 1179656 | tf_op jit(solution)/shard_map/ppermute | solution.py:162
  431.1 32.0 %collective-permute-start.30 = (bf16[64,3072]{1,0:T(8,128)(2,1)S(1)}, bf16[64,3072]{1,0:T(8,128)(2,1)S(1)}, u32[]{:S(2)}, u32[]{:S(2)}) collective-permute-start(bf16[64,3072]{1,0:T(8,128)(2,1)S(1)} %get-tuple-element.12), channel_id=1, source_target_pairs={{0,4},{4,0},{8,12},{12,8},{16,20},{20,16},{24,28},{28,24},{1,5},{5... | collective-permute-start | bytes 1179656 | tf_op jit(solution)/shard_map/ppermute | solution.py:162
  432.6 30.5 %collective-permute-start.28 = (bf16[64,3072]{1,0:T(8,128)(2,1)S(1)}, bf16[64,3072]{1,0:T(8,128)(2,1)S(1)}, u32[]{:S(2)}, u32[]{:S(2)}) collective-permute-start(bf16[64,3072]{1,0:T(8,128)(2,1)S(1)} %get-tuple-element.13), channel_id=1, source_target_pairs={{0,16},{4,20},{8,24},{12,28},{16,0},{20,4},{24,8},{28,12},{1,17},{... | collective-permute-start | bytes 1179656 | tf_op jit(solution)/shard_map/ppermute | solution.py:162
  (20 other events, 348.8 us)
Sparse Core Ops, SparseCore 0:
  10.5 35.0 all-gather.5
  48.0 32.3 all-gather.3
  82.8 45.5 all-gather.7
  370.3 62.4 reduce-scatter.1
